TPU v7x, 128 devices: a whole 4x4x4 slice. The times are simulated.
128 devices in a mesh: replica: 16 (over y, z_hi, core), fsdp: 8 (over x, z_lo).
Axes of the slice: x: 4, y: 4, z: 4 (z_hi: 2, z_lo: 2; z = z_hi * 2 + z_lo), core: 2. Of those that a mesh axis runs over, the one named last changes fastest.
Arguments:
- tokens: bfloat16 [16, 3072, 8192], P('replica', 'fsdp'), may hold values from -6 to 6
- queries: bfloat16 [16, 3072, 4096], P('replica', 'fsdp'), may hold values from -250 to 250
- kv_weight: bfloat16 [16, 8192, 1024], P('replica', 'fsdp'), may hold values from -0.06629126 to 0.06629126
- doc_lengths: int32 [16, 8, 6], P('replica', 'fsdp'), may hold values from 1 to 192, 384 in all within a row
- local_params: bfloat16 [16, 1536, 8192], P('replica', 'fsdp'), may hold values from -6 to 6
- base_copy: bfloat16 [1536, 8192], P('fsdp'), may hold values from -6 to 6
- master: float32 [1536, 8192], P('fsdp', 'replica'), may hold values from -6 to 6
- momentum: float32 [1536, 8192], P('fsdp', 'replica'), may hold values from -2 to 2
Outputs:
- attended: bfloat16 [16, 3072, 4096], P('replica', 'fsdp')
- new_master: float32 [1536, 8192], P('fsdp', 'replica')
- new_momentum: float32 [1536, 8192], P('fsdp', 'replica')
- fresh_params: bfloat16 [1536, 8192], P('fsdp')
Inputs may be any that keep to these rules, and one draw needn't show every extreme that they name: `doc_lengths`: each device's 6 lengths sum to 384, and the longest is exactly 192.
All inputs are finite; a program needn't handle non-finite values.
Results may differ from a plain program's by a relative error of at most 0.012.
The roundings to bfloat16 on the way count: a program that leaves them out, or rounds other values in their place, can miss the bound.
Values may be sent and summed in bfloat16 or wider, within the bound.
A program may use at most 192 MiB of HBM per device.

v0:
```python
import jax
import jax.numpy as jnp
from jax import lax
from jax.sharding import Mesh
from jax.sharding import PartitionSpec as P

HEAD_SIZE = 128
BLK = 128
FSDP = ("fsdp_0", "fsdp_1")


MOMENTUM_COEF = 0.9
OUTER_RATE = 0.7
QUANT_RANGE = 448.0


def summed_rows(total, axes):
    for axis in axes:
        total = lax.psum_scatter(total, axis, scatter_dimension=0, tiled=True)
    return total


def doc_mask(lengths, tok_count):
    doc_ends = jnp.cumsum(lengths)
    places = jnp.arange(tok_count, dtype=jnp.int32)
    doc_index = jnp.sum((places[:, None] >= doc_ends[None, :-1]).astype(jnp.int32), axis=1)
    same_doc = doc_index[:, None] == doc_index[None, :]
    return jnp.logical_and(same_doc, places[None, :] <= places[:, None])


def attend(query_rows, packed, lengths):
    tok_count = query_rows.shape[0]
    head_count = query_rows.shape[1] // HEAD_SIZE
    groups = packed.shape[1] // (2 * HEAD_SIZE)
    key_heads = packed[:, : groups * HEAD_SIZE].reshape(tok_count, groups, HEAD_SIZE)
    value_heads = packed[:, groups * HEAD_SIZE :].reshape(tok_count, groups, HEAD_SIZE)
    grouped = query_rows.reshape(tok_count, groups, head_count // groups, HEAD_SIZE)
    scores = jnp.einsum(
        "tgjd,sgd->gjts", grouped, key_heads, preferred_element_type=jnp.float32
    ) * HEAD_SIZE ** (-0.5)
    allowed = doc_mask(lengths, tok_count)
    scores = jnp.where(allowed[None, None], scores, -1e30)
    highest = jnp.max(scores, axis=-1, keepdims=True)
    expo = jnp.exp(scores - highest)
    attn_weights = (expo / jnp.sum(expo, axis=-1, keepdims=True)).astype(jnp.bfloat16)
    mixed = jnp.einsum(
        "gjts,sgd->tgjd", attn_weights, value_heads, preferred_element_type=jnp.float32
    )
    return mixed.reshape(tok_count, head_count * HEAD_SIZE).astype(jnp.bfloat16)


def shards(tokens, queries, kv_weight, doc_lengths, local_params, base_copy, master, momentum):
    own_tokens = tokens[0]
    own_queries = queries[0]
    lengths = doc_lengths[0, 0]
    columns = lax.all_to_all(own_tokens, FSDP, split_axis=1, concat_axis=0, tiled=True)
    weight_shard = kv_weight[0]
    packed = summed_rows(jnp.dot(columns, weight_shard, preferred_element_type=jnp.float32), FSDP)
    attended = attend(own_queries, packed.astype(jnp.bfloat16), lengths)[None]
    replicas = lax.axis_size("replica")
    row_count = base_copy.shape[0]
    full_width = base_copy.shape[1]
    block_count = full_width // BLK
    pseudo_grad = base_copy.astype(jnp.float32) - local_params[0].astype(jnp.float32)
    blocked = pseudo_grad.reshape(row_count, block_count, BLK)
    scales = ((jnp.max(jnp.abs(blocked), axis=-1) + 1e-06) / QUANT_RANGE).astype(jnp.bfloat16)
    encoded = (blocked / scales.astype(jnp.float32)[..., None]).astype(jnp.bfloat16)
    decoded = (encoded.astype(jnp.float32) * scales.astype(jnp.float32)[..., None]).reshape(
        row_count, full_width
    )
    summed = lax.psum_scatter(
        decoded.astype(jnp.bfloat16), "replica", scatter_dimension=1, tiled=True
    ).astype(jnp.float32)
    averaged = summed * (1.0 / replicas)
    new_momentum = MOMENTUM_COEF * momentum + averaged
    new_master = master - OUTER_RATE * (averaged + MOMENTUM_COEF * new_momentum)
    fresh_params = lax.all_gather(new_master.astype(jnp.bfloat16), "replica", axis=1, tiled=True)
    return (attended, new_master, new_momentum, fresh_params)


def solution(mesh):
    finer = Mesh(mesh.devices.reshape(mesh.shape["replica"], 4, 2), ("replica", "fsdp_0", "fsdp_1"))
    placed = (
        P("replica", FSDP, None),
        P("replica", FSDP, None),
        P("replica", FSDP, None),
        P("replica", FSDP, None),
        P("replica", FSDP, None),
        P(FSDP, None),
        P(FSDP, "replica"),
        P(FSDP, "replica"),
    )
    return jax.shard_map(
        shards,
        mesh=finer,
        in_specs=placed,
        out_specs=(P("replica", FSDP, None), P(FSDP, "replica"), P(FSDP, "replica"), P(FSDP, None)),
        check_vma=False,
    )
```

profile of v0, /device:TPU:0, one launch (start us, length us, event | category | flops | bytes accessed | tf_op | source)
XLA Modules:
  0.0 412.5 jit_solution(16304995047222612006)
XLA Ops:
  7.2 8.8 %copy.29 = bf16[1,384,8192]{1,2,0:T(8,128)(2,1)} copy(bf16[1,384,8192]{2,1,0:T(8,128)(2,1)} %param.8) | data formatting | bytes 12582912 | tf_op args[0]
  16.0 5.7 %all-to-all-start = ((bf16[384,8,1024]{0,2,1:T(8,128)(2,1)}), bf16[384,8,1024]{0,2,1:T(8,128)(2,1)}, u32[]{:S(2)}, u32[]{:S(2)}) async-start(bf16[384,8,1024]{0,2,1:T(8,128)(2,1)} %bitcast.52), calls=%async_computation | async-start | bytes 12582912 | tf_op jit(solution)/shard_map/all_to_all | solution.py:56
  21.8 4.0 abs_bitcast_fusion
  25.7 3.8 copy.43
  29.5 4.5 %reduce_max.19 = f32[192,64]{1,0:T(8,128)S(1)} reduce(f32[192,64,128]{2,1,0:T(8,128)} %bitcast.53, f32[]{:T(128)} %constant.5.clone.1), dimensions={2}, to_apply=%region_6.7 | reduce | flops 1560576 | bytes 6340612 | tf_op jit(solution)/shard_map/reduce_max | solution.py:66
  34.1 1.8 div.29
  35.8 0.1 copy-done.2
  35.9 1.0 copy-done.3
  36.9 6.5 %fusion.7 = bf16[192,8192]{1,0:T(8,128)(2,1)} fusion(bf16[192,8192]{1,0:T(8,128)(2,1)S(1)} %copy-done.2, f32[24,8,64,128]{3,2,1,0:T(8,128)S(1)} %bitcast.54, bf16[1,192,8192]{2,1,0:T(8,128)(2,1)S(1)} %copy-done.3), kind=kLoop, calls=%fused_computation.12 | loop fusion | flops 12582912 | bytes 15728640 | tf_op jit(solution)/shard_map/convert_element_type | solution.py:72
  43.4 0.0 reduce-scatter.4.cloned.1.call-start
  43.5 66.0 %all-to-all-done = bf16[384,8,1024]{0,2,1:T(8,128)(2,1)} async-done(((bf16[384,8,1024]{0,2,1:T(8,128)(2,1)}), bf16[384,8,1024]{0,2,1:T(8,128)(2,1)}, u32[]{:S(2)}, u32[]{:S(2)}) %all-to-all-start) | async-done | bytes 6291488 | tf_op jit(solution)/shard_map/all_to_all | solution.py:56
  109.5 8.7 %copy.30 = bf16[8,384,1024]{2,1,0:T(8,128)(2,1)} copy(bf16[8,384,1024]{1,2,0:T(8,128)(2,1)} %bitcast.1) | data formatting | bytes 12582912 | tf_op jit(solution)/shard_map/all_to_all | solution.py:56
  118.2 12.3 %fusion.11 = f32[3072,1024]{1,0:T(8,128)} fusion(bf16[3072,1024]{1,0:T(8,128)(2,1)} %bitcast.56, bf16[1,1024,1024]{2,1,0:T(8,128)(2,1)S(1)} %copy-done), kind=kOutput, calls=%fused_computation.18 | convolution fusion | flops 6442450944 | bytes 20971520 | tf_op jit(solution)/shard_map/dot_general | solution.py:58
  130.5 0.2 all-gather.2.cloned.1.call-start
  130.8 1.7 reduce-scatter.8.cloned.1.call-done
  132.5 2.0 fusion.18
  134.6 113.6 %reduce-scatter.4.cloned.1.call-done = f32[768,1024]{1,0:T(8,128)} async-done(((f32[3072,1024]{1,0:T(8,128)}), f32[768,1024]{1,0:T(8,128)}) %reduce-scatter.4.cloned.1.call-update) | async-done | bytes 3145744 | tf_op jit(solution)/shard_map/reduce_scatter | solution.py:19
  248.2 4.4 %copy.42 = bf16[48,8,32,128]{3,2,1,0:T(8,128)(2,1)} copy(bf16[48,8,32,128]{3,1,2,0:T(8,128)(2,1)} %bitcast.57) | data formatting | bytes 6291456
  252.6 0.2 reduce-window.4
  252.8 0.1 convert_reduce_fusion
  252.9 0.1 fusion.13
  253.0 52.1 %all-gather.2.cloned.1.call-done = bf16[192,8192]{1,0:T(8,128)(2,1)} async-done(((bf16[192,512]{1,0:T(8,128)(2,1)}), bf16[192,8192]{1,0:T(8,128)(2,1)}) %all-gather.2.cloned.1.call-update) | async-done | bytes 3145744 | tf_op jit(solution)/shard_map/all_gather | solution.py:77
  305.1 46.7 %reduce-scatter.6.cloned.1.call-done = f32[384,1024]{1,0:T(8,128)} async-done(((f32[768,1024]{1,0:T(8,128)}), f32[384,1024]{1,0:T(8,128)}) %reduce-scatter.6.cloned.1.call-update) | async-done | bytes 1572880 | tf_op jit(solution)/shard_map/reduce_scatter | solution.py:19
  351.8 1.5 convert_element_type.66
  353.3 0.1 fusion.19
  353.4 0.2 copy.39
  353.6 0.1 reshape.95
  353.7 11.2 %fusion.8 = f32[4,384,384,8]{2,1,3,0:T(8,128)} fusion(bf16[384,4,8,128]{3,2,1,0:T(8,128)(2,1)} %bitcast.55, bf16[384,4,128,1]{2,1,0,3:T(4,128)(2,1)S(1)} %bitcast.59), kind=kOutput, calls=%fused_computation.15 | convolution fusion | flops 1207959552 | bytes 22413312 | tf_op jit(solution)/shard_map/tgjd,sgd->gjts/dot_general | solution.py:38
  364.9 22.6 %fusion.20 = (f32[4,8,384]{2,1,0:T(8,128)S(1)}, f32[4,8,384,384]{2,3,1,0:T(8,128)}) fusion(f32[4,384,384,8]{2,1,3,0:T(8,128)} %fusion.8, pred[384,384]{0,1:T(8,128)(4,1)S(1)} %fusion.13), kind=kOutput, calls=%fused_computation.35 | output fusion | flops 28311936 | bytes 37945344 | tf_op jit(solution)/shard_map/sub | solution.py:44
  387.5 9.8 %fusion.10 = bf16[4,128,8,384]{3,1,2,0:T(8,128)(2,1)} fusion(bf16[384,4,128,1]{0,2,3,1:T(8,128)(2,1)S(1)} %bitcast.60, f32[4,8,384,384]{2,3,1,0:T(8,128)} %get-tuple-element.26, f32[4,8,384]{2,1,0:T(8,128)S(1)} %get-tuple-element.25), kind=kOutput, calls=%fused_computation.17 | convolution fusion | flops 1218969600 | bytes 22462464 | tf_op jit(solution)/shard_map/gjts,sgd->tgjd/dot_general | solution.py:46
  397.4 4.8 %copy.35 = bf16[1,384,4096]{2,1,0:T(8,128)(2,1)} copy(bf16[1,384,4096]{1,2,0:T(8,128)(2,1)} %bitcast.58) | data formatting | bytes 6291456
  402.1 3.9 copy.51
  (20 shorter events, 0.2 us)
Async XLA Ops:
  7.2 111.0 %copy-start = (bf16[1,1024,1024]{2,1,0:T(8,128)(2,1)S(1)}, bf16[1,1024,1024]{2,1,0:T(8,128)(2,1)}, u32[]{:S(2)}) copy-start(bf16[1,1024,1024]{2,1,0:T(8,128)(2,1)} %param.10) | copy-start | bytes 6291460
  16.0 93.5 %all-to-all-start = ((bf16[384,8,1024]{0,2,1:T(8,128)(2,1)}), bf16[384,8,1024]{0,2,1:T(8,128)(2,1)}, u32[]{:S(2)}, u32[]{:S(2)}) async-start(bf16[384,8,1024]{0,2,1:T(8,128)(2,1)} %bitcast.52), calls=%async_computation | async-start | bytes 12582912 | tf_op jit(solution)/shard_map/all_to_all | solution.py:56
  21.7 110.8 %reduce-scatter.8.cloned.1.call-start = ((), (), s32[]{:S(2)}) async-start(), calls=%async_computation.6 | async-start | bytes 3342336 | tf_op jit(solution)/shard_map/reduce_scatter | solution.py:71
  34.0 1.9 copy-start.2
  34.0 2.8 copy-start.3
  43.4 204.7 %reduce-scatter.4.cloned.1.call-start = ((), (), s32[]{:S(2)}) async-start(), calls=%async_computation.4 | async-start | bytes 15728640 | tf_op jit(solution)/shard_map/reduce_scatter | solution.py:19
  130.5 2.0 copy-start.4
  130.5 2.0 copy-start.5
  130.5 122.1 %copy-start.6 = (s32[1,1,6]{2,1,0:T(1,128)S(1)}, s32[1,1,6]{2,1,0:T(1,128)}, u32[]{:S(2)}) copy-start(s32[1,1,6]{2,1,0:T(1,128)} %param.11) | copy-start | bytes 76
  130.5 174.5 %all-gather.2.cloned.1.call-start = ((), (), s32[]{:S(2)}) async-start(), calls=%async_computation.7 | async-start | bytes 3342336 | tf_op jit(solution)/shard_map/all_gather | solution.py:77
  134.5 217.3 %reduce-scatter.6.cloned.1.call-start = ((), (), s32[]{:S(2)}) async-start(), calls=%async_computation.5 | async-start | bytes 4718592 | tf_op jit(solution)/shard_map/reduce_scatter | solution.py:19
  397.4 8.6 %copy-start.1 = (bf16[1,1024,1024]{2,1,0:T(8,128)(2,1)S(1)}, bf16[1,1024,1024]{2,1,0:T(8,128)(2,1)}, u32[]{:S(2)}) copy-start(bf16[1,1024,1024]{2,1,0:T(8,128)(2,1)} %param.10) | copy-start | bytes 6291460
Sparse Core Ops, SparseCore 0:
  43.5 88.9 reduce-scatter.7
  134.9 113.1 reduce-scatter.3
  251.0 54.0 all-gather.1
  307.3 44.4 reduce-scatter.5
where the time goes:
time: 414 us; the launch traced here: 413 us
  waiting for transfers between devices  280 us (68%)
  other arithmetic  41.5 us (10%)
  local copies, waits for them, and re-layouts  37.5 us (9%)
  matrix products  33.4 us (8%)
  between operations  13.9 us (3%)
  starting transfers between devices  6.08 us (1%)
    reduce_scatter x2, waiting for transfers between devices, summed_rows(): total = lax.psum_scatter(total, axis, scatter_dimension=0, tiled=True)  160 us
    all_to_all x1, waiting for transfers between devices, shards(): lax.all_to_all(own_tokens, FSDP, split_axis=1, concat_axis=0, tiled=True)  66 us
    all_gather x1, waiting for transfers between devices, shards(): lax.all_gather(new_master.astype(jnp.bfloat16), 'replica', axis=1, tiled=...  52.1 us
    unnamed x19, local copies, waits for them, and re-layouts  26.7 us
    sub x1, other arithmetic, attend(): expo = jnp.exp(scores - highest)  22.6 us
    dot_general x1, matrix products, shards(): jnp.dot(columns, weight_shard, preferred_element_type=jnp.float32)  12.3 us
    dot_general x1, matrix products, attend(): jnp.einsum('tgjd,sgd->gjts', grouped, key_heads, preferred_element_type=j...  11.2 us
    dot_general x1, matrix products, attend(): jnp.einsum('gjts,sgd->tgjd', attn_weights, value_heads, preferred_element...  9.84 us
  transfers between devices with their start and end apart: 5, of which 5 were waited for; matrix products, arithmetic and copies ran while one was open for 12% of the time, Pallas kernels for 0%

commit v1 on v0

v1 whole, which is shorter than its diff:
```python
import jax
import jax.numpy as jnp
from jax import lax
from jax.experimental import pallas as pl
from jax.experimental.pallas import tpu as pltpu
from jax.sharding import PartitionSpec as P

MESH = pl.DeviceIdType.MESH
HEAD = 128
BLK = 128
MOMENTUM_COEF = 0.9
OUTER_RATE = 0.7
QUANT_RANGE = 448.0

X = 4
Y = 4
FIRST = 448
BF = jnp.bfloat16
F32 = jnp.float32


def kernel(
    tok_h, q_h, w_h, len_s, loc_h, base_h, mast_h, mom_h,
    att_o, nmast_o, nmom_o, fresh_o,
    wbuf, tok, q, att, loc, base, csend, crecv, ysend, yrecv, zsend, zrecv, zown, mast, mom, fbuf, acc, bias,
    kv_send, kv_recv, c_send, c_recv, y_send, y_recv, z_send, z_recv, fz_send, fz_recv, fy_send, fy_recv,
    fc_send, fc_recv, w_sem, in_sem, att_sem, fo_sem, st_sem,
):
    groups = wbuf.shape[0]
    tokens = tok.shape[0]
    shard = w_h.shape[0]
    rows, owned = mast.shape
    pairs = csend.shape[0]
    per_group = q.shape[1] // HEAD // groups
    second = shard - FIRST
    half2 = second // 2

    f = lax.axis_index("fsdp")
    r = lax.axis_index("replica")
    x, z = f // 2, f % 2
    y, zh, core = r // 4, (r // 2) % 2, r % 2

    def place(dx, dz):
        return ((x + dx + X) % X) * 2 + (z + dz) % 2

    def outer(dy, dz, dc):
        return (((y + dy) % Y) * 2 + (zh + dz) % 2) * 2 + (core + dc) % 2

    right = {"fsdp": place(1, 0)}
    left = {"fsdp": place(-1, 0)}
    across = {"fsdp": place(0, 1)}
    twin = {"replica": outer(0, 0, 1)}
    ypeers = [{"replica": outer(d, 0, 0)} for d in range(1, Y)]
    far = {"replica": outer(0, 1, 0)}

    barrier = pltpu.get_barrier_semaphore()
    peers = [right, left, across, twin, far] + ypeers
    for peer in peers:
        pl.semaphore_signal(barrier, inc=1, device_id=peer, device_id_type=MESH)

    def w_copy(g, side):
        return pltpu.make_async_copy(
            w_h.at[:, pl.ds(pl.multiple_of((side * groups + g) * HEAD, HEAD), HEAD)],
            wbuf.at[g, pl.ds(pl.multiple_of(f * shard, 16), shard), pl.ds(side * HEAD, HEAD)],
            w_sem.at[g, side],
        )

    loads = [
        pltpu.make_async_copy(a, b, in_sem.at[i])
        for i, (a, b) in enumerate(
            ((loc_h, loc), (base_h, base), (tok_h, tok), (q_h, q), (mast_h, mast), (mom_h, mom))
        )
    ]
    for g in range(groups):
        for side in range(2):
            w_copy(g, side).start()
    for load in loads:
        load.start()

    kinds = (
        (place(0, 0), FIRST, second, across, place(0, 1)),
        (place(0, 0), 0, FIRST, across, place(0, 1)),
        (place(0, 0), 0, shard, right, place(-1, 0)),
        (place(0, 0), 0, shard, left, place(1, 0)),
        (place(0, 1), FIRST, second, right, place(-1, 1)),
        (place(0, 1), FIRST, second, left, place(1, 1)),
        (place(-1, 0), 0, shard // 2, right, place(2, 0)),
        (place(1, 0), shard // 2, shard // 2, left, place(2, 0)),
        (place(-1, 0), 0, FIRST, across, place(-1, 1)),
        (place(1, 0), 0, FIRST, across, place(1, 1)),
        (place(-1, 1), FIRST, half2, right, place(2, 1)),
        (place(1, 1), FIRST + half2, half2, left, place(2, 1)),
        (place(2, 0), 0, FIRST, across, place(2, 1)),
    )

    def moved(k, g, arriving):
        source, start, count, target, other = kinds[k]
        held = other if arriving else source
        part = wbuf.at[g, pl.ds(pl.multiple_of(held * shard + start, 16), count), :]
        return pltpu.make_async_remote_copy(
            src_ref=part,
            dst_ref=part,
            send_sem=kv_send.at[g, k],
            recv_sem=kv_recv.at[g, k],
            device_id=target,
            device_id_type=MESH,
        )

    def send(g, *which):
        for k in which:
            moved(k, g, False).start()

    def arrived(g, *which):
        for k in which:
            moved(k, g, True).wait_recv()

    def own(g):
        w_copy(g, 0).wait()
        w_copy(g, 1).wait()
        send(g, 0, 2, 3, 1)

    pl.semaphore_wait(barrier, len(peers))
    own(0)
    own(1)

    ends = []
    total = len_s[0]
    for i in range(len_s.shape[0] - 1):
        ends.append(total)
        total = total + len_s[i + 1]
    row_at = lax.broadcasted_iota(jnp.int32, (tokens, 1), 0)
    col_at = lax.broadcasted_iota(jnp.int32, (1, tokens), 1)
    row_doc = jnp.zeros((tokens, 1), jnp.int32)
    col_doc = jnp.zeros((1, tokens), jnp.int32)
    for end in ends:
        row_doc += (row_at >= end).astype(jnp.int32)
        col_doc += (col_at >= end).astype(jnp.int32)
    allowed = jnp.logical_and(row_doc == col_doc, col_at <= row_at)
    bias[...] = jnp.where(allowed, 0.0, -1e30).astype(F32)

    tile = 32

    def decoded(row, col):
        grad = base[pl.ds(row, tile), pl.ds(col, BLK)].astype(F32) - loc[pl.ds(row, tile), pl.ds(col, BLK)].astype(F32)
        top = jnp.max(jnp.abs(grad), axis=1, keepdims=True)
        scale = ((top + 1e-6) / QUANT_RANGE).astype(BF).astype(F32)
        return (grad / scale).astype(BF).astype(F32) * scale

    def over_block(j, side, store):
        first = pl.multiple_of((2 * j + side) * owned, owned)

        def step(t, carry):
            row = pl.multiple_of(t * tile, tile)
            for b in range(owned // BLK):
                store(row, b * BLK, decoded(row, pl.multiple_of(first + b * BLK, BLK)))
            return carry

        lax.fori_loop(0, rows // tile, step, 0)

    def c_copy(j):
        return pltpu.make_async_remote_copy(
            src_ref=csend.at[j], dst_ref=crecv.at[j], send_sem=c_send.at[j], recv_sem=c_recv.at[j],
            device_id=twin, device_id_type=MESH,
        )

    def y_copy(d, arriving):
        part = y if arriving else (y + d) % Y
        return pltpu.make_async_remote_copy(
            src_ref=ysend.at[pl.ds(2 * part, 2)], dst_ref=yrecv.at[d - 1], send_sem=y_send.at[d - 1],
            recv_sem=y_recv.at[d - 1], device_id=ypeers[d - 1], device_id_type=MESH,
        )

    def z_copy():
        return pltpu.make_async_remote_copy(
            src_ref=zsend, dst_ref=zrecv, send_sem=z_send, recv_sem=z_recv, device_id=far, device_id_type=MESH
        )

    def fz_copy(arriving):
        part = fbuf.at[core, 2 * y + (1 - zh if arriving else zh)]
        return pltpu.make_async_remote_copy(
            src_ref=part, dst_ref=part, send_sem=fz_send, recv_sem=fz_recv, device_id=far, device_id_type=MESH
        )

    def fy_copy(d, arriving):
        part = fbuf.at[core, pl.ds(2 * ((y - d + Y) % Y if arriving else y), 2)]
        return pltpu.make_async_remote_copy(
            src_ref=part, dst_ref=part, send_sem=fy_send.at[d - 1], recv_sem=fy_recv.at[d - 1],
            device_id=ypeers[d - 1], device_id_type=MESH,
        )

    def fc_copy(d, arriving):
        at = pl.ds(2 * ((y - d + Y) % Y), 2)
        part = fbuf.at[1 - core, at] if arriving else fbuf.at[core, at]
        return pltpu.make_async_remote_copy(
            src_ref=part, dst_ref=part, send_sem=fc_send.at[d], recv_sem=fc_recv.at[d],
            device_id=twin, device_id_type=MESH,
        )

    def f_out(side, j):
        return pltpu.make_async_copy(
            fbuf.at[side, j],
            fresh_o.at[:, pl.ds(pl.multiple_of((2 * j + side) * owned, owned), owned)],
            fo_sem.at[side, j],
        )

    loads[0].wait()
    loads[1].wait()

    def for_twin(j, carry):
        def store(row, col, value):
            csend[j, pl.ds(row, tile), pl.ds(col, BLK)] = value.astype(BF)

        over_block(j, 1 - core, store)
        c_copy(j).start()
        return carry

    lax.fori_loop(0, pairs, for_twin, 0)

    def with_twin(j, carry):
        c_copy(j).wait_recv()

        def store(row, col, value):
            at = (j, pl.ds(row, tile), pl.ds(col, BLK))
            ysend[at] = (value + crecv[at].astype(F32)).astype(BF)

        over_block(j, core, store)
        return carry

    def sum_y(part, row):
        at = pl.ds(row, tile)
        value = ysend[2 * y + part, at, :].astype(F32)
        for d in range(Y - 1):
            value = value + yrecv[d, part, at, :].astype(F32)
        return value

    def row_tiles(body):
        def step(t, carry):
            body(pl.multiple_of(t * tile, tile))
            return carry

        lax.fori_loop(0, rows // tile, step, 0)

    def att_out(g):
        cols = pl.ds(pl.multiple_of(g * per_group * HEAD, HEAD), per_group * HEAD)
        return pltpu.make_async_copy(att.at[:, cols], att_o.at[:, cols], att_sem.at[g])

    nq = 3
    qrows = tokens // nq

    def compute(g):
        acc[...] = jnp.zeros_like(acc)

        def project(s, carry):
            at = pl.ds(pl.multiple_of(s * shard, shard), shard)
            acc[...] += jnp.dot(tok[:, at], wbuf[g, at, :], preferred_element_type=F32)
            return carry

        lax.fori_loop(0, wbuf.shape[1] // shard, project, 0)
        keys = acc[:, :HEAD].astype(BF)
        values = acc[:, HEAD:].astype(BF)

        def head(j, carry):
            cols = pl.ds(pl.multiple_of((g * per_group + j) * HEAD, HEAD), HEAD)
            for i in range(nq):
                at = pl.ds(i * qrows, qrows)
                seen = (i + 1) * qrows
                scores = lax.dot_general(
                    q[at, cols], keys[:seen], (((1,), (1,)), ((), ())), preferred_element_type=F32
                )
                scores = scores * HEAD**-0.5 + bias[at, :seen]
                expo = jnp.exp(scores - jnp.max(scores, axis=1, keepdims=True))
                weights = (expo / jnp.sum(expo, axis=1, keepdims=True)).astype(BF)
                att[at, cols] = jnp.dot(weights, values[:seen], preferred_element_type=F32).astype(BF)
            return carry

        lax.fori_loop(0, per_group, head, 0)
        att_out(g).start()

    def turn(g, carry):
        @pl.when(g < groups)
        def _():
            arrived(g, 0)
            send(g, 4, 5)
            arrived(g, 2)
            send(g, 6, 8)
            arrived(g, 3)
            send(g, 7, 9)

        @pl.when(g + 2 < groups)
        def _():
            own(g + 2)

        @pl.when(g < groups)
        def _():
            arrived(g, 4)
            send(g, 10)
            arrived(g, 5)
            send(g, 11)
            arrived(g, 6)
            send(g, 12)

        @pl.when(g == 0)
        def _():
            lax.fori_loop(0, pairs, with_twin, 0)
            for d in range(1, Y):
                y_copy(d, False).start()
            loads[2].wait()
            loads[3].wait()
            loads[4].wait()
            loads[5].wait()

        @pl.when(g == 1)
        def _():
            for d in range(1, Y):
                y_copy(d, True).wait_recv()

            def body(row):
                zsend[pl.ds(row, tile), :] = sum_y(1 - zh, row).astype(BF)
                zown[pl.ds(row, tile), :] = sum_y(zh, row)

            row_tiles(body)
            z_copy().start()

        @pl.when(g == 2)
        def _():
            z_copy().wait_recv()

            def body(row):
                at = pl.ds(row, tile)
                averaged = (zown[at, :] + zrecv[at, :].astype(F32)) * (1.0 / 16)
                moved_on = MOMENTUM_COEF * mom[at, :] + averaged
                updated = mast[at, :] - OUTER_RATE * (averaged + MOMENTUM_COEF * moved_on)
                mom[at, :] = moved_on
                mast[at, :] = updated
                fbuf[core, 2 * y + zh, at, :] = updated.astype(BF)

            row_tiles(body)
            fz_copy(False).start()
            pltpu.make_async_copy(mom, nmom_o, st_sem.at[0]).start()
            pltpu.make_async_copy(mast, nmast_o, st_sem.at[1]).start()

        @pl.when(g == 3)
        def _():
            fz_copy(True).wait_recv()
            for d in range(1, Y):
                fy_copy(d, False).start()
            fc_copy(0, False).start()

        @pl.when(g == groups)
        def _():
            for d in range(1, Y):
                fy_copy(d, True).wait_recv()
                fc_copy(d, False).start()

        @pl.when(g > 0)
        def _():
            arrived(g - 1, 1, 7, 8, 9, 10, 11, 12)
            compute(g - 1)

        return carry

    lax.fori_loop(0, groups + 1, turn, 0)

    def out_own(j, carry):
        f_out(core, j).start()
        return carry

    lax.fori_loop(0, pairs, out_own, 0)
    for d in range(Y):
        fc_copy(d, True).wait_recv()

    def out_twin(j, carry):
        f_out(1 - core, j).start()
        return carry

    lax.fori_loop(0, pairs, out_twin, 0)

    def sent(g, carry):
        for k in range(len(kinds)):
            moved(k, g, False).wait_send()
        att_out(g).wait()
        return carry

    lax.fori_loop(0, groups, sent, 0)

    def c_sent(j, carry):
        c_copy(j).wait_send()
        f_out(0, j).wait()
        f_out(1, j).wait()
        return carry

    lax.fori_loop(0, pairs, c_sent, 0)
    for d in range(1, Y):
        y_copy(d, False).wait_send()
        fy_copy(d, False).wait_send()
    for d in range(Y):
        fc_copy(d, False).wait_send()
    z_copy().wait_send()
    fz_copy(False).wait_send()
    pltpu.make_async_copy(mom, nmom_o, st_sem.at[0]).wait()
    pltpu.make_async_copy(mast, nmast_o, st_sem.at[1]).wait()


def shards(tokens, queries, kv_weight, doc_lengths, local_params, base_copy, master, momentum):
    tok_count, width = tokens.shape[1:]
    q_width = queries.shape[2]
    shard, kv_width = kv_weight.shape[1:]
    rows, full = base_copy.shape
    owned = master.shape[1]
    groups = kv_width // (2 * HEAD)
    pairs = full // owned // 2
    hbm = pl.BlockSpec(memory_space=pl.ANY)
    dma = pltpu.SemaphoreType.DMA
    outs = pl.pallas_call(
        kernel,
        out_shape=(
            jax.ShapeDtypeStruct((tok_count, q_width), BF),
            jax.ShapeDtypeStruct((rows, owned), F32),
            jax.ShapeDtypeStruct((rows, owned), F32),
            jax.ShapeDtypeStruct((rows, full), BF),
        ),
        in_specs=[hbm] * 3 + [pl.BlockSpec(memory_space=pltpu.SMEM)] + [hbm] * 4,
        out_specs=(hbm,) * 4,
        scratch_shapes=[
            pltpu.VMEM((groups, width, 2 * HEAD), BF),
            pltpu.VMEM((tok_count, width), BF),
            pltpu.VMEM((tok_count, q_width), BF),
            pltpu.VMEM((tok_count, q_width), BF),
            pltpu.VMEM((rows, full), BF),
            pltpu.VMEM((rows, full), BF),
            pltpu.VMEM((pairs, rows, owned), BF),
            pltpu.VMEM((pairs, rows, owned), BF),
            pltpu.VMEM((pairs, rows, owned), BF),
            pltpu.VMEM((Y - 1, 2, rows, owned), BF),
            pltpu.VMEM((rows, owned), BF),
            pltpu.VMEM((rows, owned), BF),
            pltpu.VMEM((rows, owned), F32),
            pltpu.VMEM((rows, owned), F32),
            pltpu.VMEM((rows, owned), F32),
            pltpu.VMEM((2, pairs, rows, owned), BF),
            pltpu.VMEM((tok_count, 2 * HEAD), F32),
            pltpu.VMEM((tok_count, tok_count), F32),
            dma((groups, 13)),
            dma((groups, 13)),
            dma((pairs,)),
            dma((pairs,)),
            dma((Y - 1,)),
            dma((Y - 1,)),
            dma,
            dma,
            dma,
            dma,
            dma((Y - 1,)),
            dma((Y - 1,)),
            dma((Y,)),
            dma((Y,)),
            dma((groups, 2)),
            dma((6,)),
            dma((groups,)),
            dma((2, pairs)),
            dma((2,)),
        ],
        compiler_params=pltpu.CompilerParams(
            collective_id=0, has_side_effects=True, vmem_limit_bytes=60 * 1024 * 1024
        ),
        cost_estimate=pl.CostEstimate(flops=9 * 10**9, bytes_accessed=3 * 10**7, transcendentals=5 * 10**6),
        name="fused",
    )(
        tokens[0], queries[0], kv_weight[0], doc_lengths[0, 0], local_params[0], base_copy, master, momentum
    )
    attended, new_master, new_momentum, fresh = outs
    return attended[None], new_master, new_momentum, fresh


def solution(mesh):
    return jax.shard_map(
        shards,
        mesh=mesh,
        in_specs=(
            P("replica", "fsdp", None),
            P("replica", "fsdp", None),
            P("replica", "fsdp", None),
            P("replica", "fsdp", None),
            P("replica", "fsdp", None),
            P("fsdp", None),
            P("fsdp", "replica"),
            P("fsdp", "replica"),
        ),
        out_specs=(P("replica", "fsdp", None), P("fsdp", "replica"), P("fsdp", "replica"), P("fsdp", None)),
        check_vma=False,
    )
```

time: 414 us -> 161 us (0.39)
  waiting for transfers between devices: 280 us -> 0 us
  Pallas kernels: 0 us -> 153 us
  other arithmetic: 41.5 us -> 0 us
  matrix products: 33.4 us -> 0 us
  local copies, waits for them, and re-layouts: 37.5 us -> 7.23 us
  between operations: 13.9 us -> 0.67 us
  starting transfers between devices: 6.08 us -> 0 us
    reduce_scatter x3 -> x0, waiting for transfers between devices: 162 us -> none  [the longest x2 160 us: summed_rows(): total = lax.psum_scatter(total, axis, scatter_dimension=0, tiled=True)]
    pallas_call x0 -> x1, Pallas kernels: none -> 153 us  [shards(): pl.pallas_call(kernel, out_shape=(jax.ShapeDtypeStruct((tok_count, q_widt...]
    all_to_all x1 -> x0, waiting for transfers between devices: 66 us -> none  [shards(): lax.all_to_all(own_tokens, FSDP, split_axis=1, concat_axis=0, tiled=True)]
    all_gather x1 -> x0, waiting for transfers between devices: 52.1 us -> none  [shards(): lax.all_gather(new_master.astype(jnp.bfloat16), 'replica', axis=1, tiled=...]
    dot_general x3 -> x0, matrix products: 33.4 us -> none  [the longest x1 12.3 us: shards(): jnp.dot(columns, weight_shard, preferred_element_type=jnp.float32)]
    sub x1 -> x0, other arithmetic: 22.6 us -> none  [attend(): expo = jnp.exp(scores - highest)]
    unnamed x19 -> x10, local copies, waits for them, and re-layouts: 26.7 us -> 7.23 us
    convert_element_type x4 -> x0, other arithmetic: 10.1 us -> none  [the longest x1 6.52 us: shards(): decoded.astype(jnp.bfloat16)]
  transfers between devices with their start and end apart: 5 -> 0, of which waited for: 5 -> 0; matrix products, arithmetic and copies ran while one was open for 12% -> 0% of each run, Pallas kernels for 0% -> 0%
where the time goes in v1:
time: 161 us
  Pallas kernels  153 us (95%)
  local copies, waits for them, and re-layouts  7.23 us (4%)
    pallas_call x1, Pallas kernels, shards(): pl.pallas_call(kernel, out_shape=(jax.ShapeDtypeStruct((tok_count, q_widt...  153 us
    unnamed x10, local copies, waits for them, and re-layouts  7.23 us

profile of v1, /device:TPU:0, one launch (start us, length us, event | category | flops | bytes accessed | tf_op | source)
XLA Modules:
  0.0 161.1 jit_solution(10019423838237707523)
XLA Ops:
  0.6 153.2 %fused.1 = (bf16[384,4096]{1,0:T(8,128)(2,1)}, f32[192,512]{1,0:T(8,128)}, f32[192,512]{1,0:T(8,128)}, bf16[192,8192]{1,0:T(8,128)(2,1)}) custom-call(bf16[384,8192]{1,0:T(8,128)(2,1)} %bitcast.7, bf16[384,4096]{1,0:T(8,128)(2,1)} %bitcast.8, bf16[1024,1024]{1,0:T(8,128)(2,1)} %bitcast.10, s32[6]{0:T(128)} %bitcast.11, bf16[192,8192]{1,0:T(8,128)(2,1)} %bitcast.9, ...), custom_call_target="tpu_custom_call" | custom-call | flops 8999999488 | bytes 30000000 | tf_op jit(solution)/shard_map/fused/pallas_call | solution.py:414
  153.9 0.0 copy-start.2
  153.9 0.0 copy-start.1
  153.9 0.0 copy-start
  153.9 4.1 %copy.16 = bf16[1,384,4096]{2,1,0:T(8,128)(2,1)} copy(bf16[1,384,4096]{2,1,0:T(8,128)(2,1)} %bitcast.6) | data formatting | bytes 6291456
  158.0 0.0 copy-done.2
  158.0 0.7 copy.17
  158.7 0.0 copy-done.1
  158.7 0.7 copy.18
  159.5 0.0 copy-done
  159.5 1.7 %copy.19 = bf16[192,8192]{1,0:T(8,128)(2,1)} copy(bf16[192,8192]{1,0:T(8,128)(2,1)S(1)} %copy-done) | data formatting | bytes 6291456
Async XLA Ops:
  153.9 4.1 %copy-start.2 = (f32[192,512]{1,0:T(8,128)S(1)}, f32[192,512]{1,0:T(8,128)}, u32[]{:S(2)}) copy-start(f32[192,512]{1,0:T(8,128)} %get-tuple-element.17) | copy-start | bytes 1179652
  153.9 4.8 %copy-start.1 = (f32[192,512]{1,0:T(8,128)S(1)}, f32[192,512]{1,0:T(8,128)}, u32[]{:S(2)}) copy-start(f32[192,512]{1,0:T(8,128)} %get-tuple-element.18) | copy-start | bytes 1179652
  153.9 5.6 %copy-start = (bf16[192,8192]{1,0:T(8,128)(2,1)S(1)}, bf16[192,8192]{1,0:T(8,128)(2,1)}, u32[]{:S(2)}) copy-start(bf16[192,8192]{1,0:T(8,128)(2,1)} %get-tuple-element.19) | copy-start | bytes 9437188

commit v2 on v1

--- a/solution.py
+++ b/solution.py
@@ -11,20 +11,21 @@
 MOMENTUM_COEF = 0.9
 OUTER_RATE = 0.7
 QUANT_RANGE = 448.0
+LOG2E = 1.4426950408889634
 
 X = 4
 Y = 4
-FIRST = 448
+FIRST = 416
 BF = jnp.bfloat16
 F32 = jnp.float32
 
 
 def kernel(
     tok_h, q_h, w_h, len_s, loc_h, base_h, mast_h, mom_h,
-    att_o, nmast_o, nmom_o, fresh_o,
-    wbuf, tok, q, att, loc, base, csend, crecv, ysend, yrecv, zsend, zrecv, zown, mast, mom, fbuf, acc, bias,
+    att, mast_o, mom_o, fresh_o,
+    wbuf, tok, q, loc, base, csend, crecv, ysend, yhalf, yrecv, zsend, zrecv, zown, mast, mom, fbuf, acc, packed, bias,
     kv_send, kv_recv, c_send, c_recv, y_send, y_recv, z_send, z_recv, fz_send, fz_recv, fy_send, fy_recv,
-    fc_send, fc_recv, w_sem, in_sem, att_sem, fo_sem, st_sem,
+    fc_send, fc_recv, w_sem, in_sem, fo_sem,
 ):
     groups = wbuf.shape[0]
     tokens = tok.shape[0]
@@ -44,13 +45,13 @@
         return ((x + dx + X) % X) * 2 + (z + dz) % 2
 
     def outer(dy, dz, dc):
-        return (((y + dy) % Y) * 2 + (zh + dz) % 2) * 2 + (core + dc) % 2
+        return (((y + dy + Y) % Y) * 2 + (zh + dz) % 2) * 2 + (core + dc) % 2
 
     right = {"fsdp": place(1, 0)}
     left = {"fsdp": place(-1, 0)}
     across = {"fsdp": place(0, 1)}
     twin = {"replica": outer(0, 0, 1)}
-    ypeers = [{"replica": outer(d, 0, 0)} for d in range(1, Y)]
+    ypeers = [{"replica": outer(d, 0, 0)} for d in (1, -1)]
     far = {"replica": outer(0, 1, 0)}
 
     barrier = pltpu.get_barrier_semaphore()
@@ -163,11 +164,19 @@
             device_id=twin, device_id_type=MESH,
         )
 
-    def y_copy(d, arriving):
-        part = y if arriving else (y + d) % Y
-        return pltpu.make_async_remote_copy(
-            src_ref=ysend.at[pl.ds(2 * part, 2)], dst_ref=yrecv.at[d - 1], send_sem=y_send.at[d - 1],
-            recv_sem=y_recv.at[d - 1], device_id=ypeers[d - 1], device_id_type=MESH,
+    def ahead(d):
+        return (y + d + Y) % Y
+
+    def y_half(way):
+        return pltpu.make_async_remote_copy(
+            src_ref=ysend.at[2 * ahead(2) + way], dst_ref=yhalf.at[way], send_sem=y_send.at[way],
+            recv_sem=y_recv.at[way], device_id=ypeers[way], device_id_type=MESH,
+        )
+
+    def y_pair(way):
+        return pltpu.make_async_remote_copy(
+            src_ref=ysend.at[pl.ds(2 * ahead(1 - 2 * way), 2)], dst_ref=yrecv.at[way], send_sem=y_send.at[2 + way],
+            recv_sem=y_recv.at[2 + way], device_id=ypeers[way], device_id_type=MESH,
         )
 
     def z_copy():
@@ -181,18 +190,25 @@
             src_ref=part, dst_ref=part, send_sem=fz_send, recv_sem=fz_recv, device_id=far, device_id_type=MESH
         )
 
-    def fy_copy(d, arriving):
-        part = fbuf.at[core, pl.ds(2 * ((y - d + Y) % Y if arriving else y), 2)]
-        return pltpu.make_async_remote_copy(
-            src_ref=part, dst_ref=part, send_sem=fy_send.at[d - 1], recv_sem=fy_recv.at[d - 1],
-            device_id=ypeers[d - 1], device_id_type=MESH,
+    def f_pair(way, arriving):
+        part = fbuf.at[core, pl.ds(2 * (ahead(2 * way - 1) if arriving else y), 2)]
+        return pltpu.make_async_remote_copy(
+            src_ref=part, dst_ref=part, send_sem=fy_send.at[way], recv_sem=fy_recv.at[way],
+            device_id=ypeers[way], device_id_type=MESH,
+        )
+
+    def f_half(way, arriving):
+        part = fbuf.at[core, 2 * ahead(2 if arriving else 2 * way - 1) + way]
+        return pltpu.make_async_remote_copy(
+            src_ref=part, dst_ref=part, send_sem=fy_send.at[2 + way], recv_sem=fy_recv.at[2 + way],
+            device_id=ypeers[way], device_id_type=MESH,
         )
 
     def fc_copy(d, arriving):
-        at = pl.ds(2 * ((y - d + Y) % Y), 2)
+        at = pl.ds(2 * ahead(d), 2)
         part = fbuf.at[1 - core, at] if arriving else fbuf.at[core, at]
         return pltpu.make_async_remote_copy(
-            src_ref=part, dst_ref=part, send_sem=fc_send.at[d], recv_sem=fc_recv.at[d],
+            src_ref=part, dst_ref=part, send_sem=fc_send.at[d + 1], recv_sem=fc_recv.at[d + 1],
             device_id=twin, device_id_type=MESH,
         )
 
@@ -229,8 +245,8 @@
     def sum_y(part, row):
         at = pl.ds(row, tile)
         value = ysend[2 * y + part, at, :].astype(F32)
-        for d in range(Y - 1):
-            value = value + yrecv[d, part, at, :].astype(F32)
+        for way in range(2):
+            value = value + yrecv[way, part, at, :].astype(F32)
         return value
 
     def row_tiles(body):
@@ -240,79 +256,99 @@
 
         lax.fori_loop(0, rows // tile, step, 0)
 
-    def att_out(g):
-        cols = pl.ds(pl.multiple_of(g * per_group * HEAD, HEAD), per_group * HEAD)
-        return pltpu.make_async_copy(att.at[:, cols], att_o.at[:, cols], att_sem.at[g])
-
     nq = 3
     qrows = tokens // nq
 
     def compute(g):
-        acc[...] = jnp.zeros_like(acc)
-
-        def project(s, carry):
-            at = pl.ds(pl.multiple_of(s * shard, shard), shard)
-            acc[...] += jnp.dot(tok[:, at], wbuf[g, at, :], preferred_element_type=F32)
-            return carry
-
-        lax.fori_loop(0, wbuf.shape[1] // shard, project, 0)
-        keys = acc[:, :HEAD].astype(BF)
-        values = acc[:, HEAD:].astype(BF)
-
-        def head(j, carry):
-            cols = pl.ds(pl.multiple_of((g * per_group + j) * HEAD, HEAD), HEAD)
-            for i in range(nq):
-                at = pl.ds(i * qrows, qrows)
-                seen = (i + 1) * qrows
-                scores = lax.dot_general(
-                    q[at, cols], keys[:seen], (((1,), (1,)), ((), ())), preferred_element_type=F32
+        def part(held):
+            return jnp.dot(
+                tok[:, pl.ds(pl.multiple_of(held * shard, shard), shard)],
+                wbuf[g, pl.ds(pl.multiple_of(held * shard, shard), shard), :],
+                preferred_element_type=F32,
+            )
+
+        acc[...] = part(place(0, 0))
+        acc[...] += part(place(-1, 0))
+        acc[...] += part(place(1, 0))
+        for held, which in (
+            (place(0, 1), (1,)),
+            (place(2, 0), (7,)),
+            (place(-1, 1), (8,)),
+            (place(1, 1), (9,)),
+            (place(2, 1), (10, 11, 12)),
+        ):
+            arrived(g, *which)
+            acc[...] += part(held)
+        packed[...] = acc[...].astype(BF)
+
+        heads = [pl.ds(pl.multiple_of((g * per_group + h) * HEAD, HEAD), HEAD) for h in range(per_group)]
+        for i in range(nq):
+            at = pl.ds(i * qrows, qrows)
+            seen = (i + 1) * qrows
+            scores = [
+                lax.dot_general(
+                    q[at, cols], packed[:seen, :HEAD], (((1,), (1,)), ((), ())), preferred_element_type=F32
                 )
-                scores = scores * HEAD**-0.5 + bias[at, :seen]
-                expo = jnp.exp(scores - jnp.max(scores, axis=1, keepdims=True))
-                weights = (expo / jnp.sum(expo, axis=1, keepdims=True)).astype(BF)
-                att[at, cols] = jnp.dot(weights, values[:seen], preferred_element_type=F32).astype(BF)
-            return carry
-
-        lax.fori_loop(0, per_group, head, 0)
-        att_out(g).start()
-
-    def turn(g, carry):
-        @pl.when(g < groups)
-        def _():
-            arrived(g, 0)
-            send(g, 4, 5)
-            arrived(g, 2)
-            send(g, 6, 8)
-            arrived(g, 3)
-            send(g, 7, 9)
-
-        @pl.when(g + 2 < groups)
-        def _():
-            own(g + 2)
-
-        @pl.when(g < groups)
-        def _():
-            arrived(g, 4)
-            send(g, 10)
-            arrived(g, 5)
-            send(g, 11)
-            arrived(g, 6)
-            send(g, 12)
-
-        @pl.when(g == 0)
+                * (HEAD**-0.5 * LOG2E)
+                + bias[at, :seen]
+                for cols in heads
+            ]
+            highest = [jnp.max(s, axis=1, keepdims=True) for s in scores]
+            expo = [jnp.exp2(s - m) for s, m in zip(scores, highest)]
+            over = [1.0 / jnp.sum(e, axis=1, keepdims=True) for e in expo]
+            for cols, e, o in zip(heads, expo, over):
+                weights = (e * o).astype(BF)
+                att[at, cols] = jnp.dot(weights, packed[:seen, HEAD:], preferred_element_type=F32).astype(BF)
+
+    def turn(t, carry):
+        @pl.when(t == 1)
+        def _():
+            for way in range(2):
+                y_half(way).wait_recv()
+                onward = 2 * ahead(1 - 2 * way) + way
+
+                def body(row):
+                    at = pl.ds(row, tile)
+                    value = ysend[onward, at, :].astype(F32) + yhalf[way, at, :].astype(F32)
+                    ysend[onward, at, :] = value.astype(BF)
+
+                row_tiles(body)
+                y_pair(way).start()
+
+        @pl.when(t < groups)
+        def _():
+            arrived(t, 0)
+            send(t, 4, 5)
+            arrived(t, 2)
+            send(t, 6, 8)
+            arrived(t, 3)
+            send(t, 7, 9)
+
+        @pl.when(jnp.logical_and(t > 0, t <= groups))
+        def _():
+            arrived(t - 1, 4)
+            send(t - 1, 10)
+            arrived(t - 1, 5)
+            send(t - 1, 11)
+            arrived(t - 1, 6)
+            send(t - 1, 12)
+
+        @pl.when(t + 2 < groups)
+        def _():
+            own(t + 2)
+
+        @pl.when(t == 0)
         def _():
             lax.fori_loop(0, pairs, with_twin, 0)
-            for d in range(1, Y):
-                y_copy(d, False).start()
-            loads[2].wait()
-            loads[3].wait()
-            loads[4].wait()
-            loads[5].wait()
-
-        @pl.when(g == 1)
-        def _():
-            for d in range(1, Y):
-                y_copy(d, True).wait_recv()
+            for way in range(2):
+                y_half(way).start()
+            for load in loads[2:]:
+                load.wait()
+
+        @pl.when(t == 1)
+        def _():
+            for way in range(2):
+                y_pair(way).wait_recv()
 
             def body(row):
                 zsend[pl.ds(row, tile), :] = sum_y(1 - zh, row).astype(BF)
@@ -321,7 +357,34 @@
             row_tiles(body)
             z_copy().start()
 
-        @pl.when(g == 2)
+        @pl.when(t == 3)
+        def _():
+            fz_copy(True).wait_recv()
+            for way in range(2):
+                f_pair(way, False).start()
+            fc_copy(0, False).start()
+
+        @pl.when(t == groups + 1)
+        def _():
+            def out_own(j, carry):
+                f_out(core, j).start()
+                return carry
+
+            lax.fori_loop(0, pairs, out_own, 0)
+            for d in range(-1, Y - 1):
+                fc_copy(d, True).wait_recv()
+
+            def out_twin(j, carry):
+                f_out(1 - core, j).start()
+                return carry
+
+            lax.fori_loop(0, pairs, out_twin, 0)
+
+        @pl.when(t > 1)
+        def _():
+            compute(t - 2)
+
+        @pl.when(t == 2)
         def _():
             z_copy().wait_recv()
 
@@ -330,55 +393,33 @@
                 averaged = (zown[at, :] + zrecv[at, :].astype(F32)) * (1.0 / 16)
                 moved_on = MOMENTUM_COEF * mom[at, :] + averaged
                 updated = mast[at, :] - OUTER_RATE * (averaged + MOMENTUM_COEF * moved_on)
-                mom[at, :] = moved_on
-                mast[at, :] = updated
+                mom_o[at, :] = moved_on
+                mast_o[at, :] = updated
                 fbuf[core, 2 * y + zh, at, :] = updated.astype(BF)
 
             row_tiles(body)
             fz_copy(False).start()
-            pltpu.make_async_copy(mom, nmom_o, st_sem.at[0]).start()
-            pltpu.make_async_copy(mast, nmast_o, st_sem.at[1]).start()
-
-        @pl.when(g == 3)
-        def _():
-            fz_copy(True).wait_recv()
-            for d in range(1, Y):
-                fy_copy(d, False).start()
-            fc_copy(0, False).start()
-
-        @pl.when(g == groups)
-        def _():
-            for d in range(1, Y):
-                fy_copy(d, True).wait_recv()
-                fc_copy(d, False).start()
-
-        @pl.when(g > 0)
-        def _():
-            arrived(g - 1, 1, 7, 8, 9, 10, 11, 12)
-            compute(g - 1)
+
+        @pl.when(t == 3)
+        def _():
+            for way in range(2):
+                f_pair(way, True).wait_recv()
+                f_half(way, False).start()
+                fc_copy(2 * way - 1, False).start()
+
+        @pl.when(t == groups)
+        def _():
+            for way in range(2):
+                f_half(way, True).wait_recv()
+            fc_copy(2, False).start()
 
         return carry
 
-    lax.fori_loop(0, groups + 1, turn, 0)
-
-    def out_own(j, carry):
-        f_out(core, j).start()
-        return carry
-
-    lax.fori_loop(0, pairs, out_own, 0)
-    for d in range(Y):
-        fc_copy(d, True).wait_recv()
-
-    def out_twin(j, carry):
-        f_out(1 - core, j).start()
-        return carry
-
-    lax.fori_loop(0, pairs, out_twin, 0)
+    lax.fori_loop(0, groups + 2, turn, 0)
 
     def sent(g, carry):
         for k in range(len(kinds)):
             moved(k, g, False).wait_send()
-        att_out(g).wait()
         return carry
 
     lax.fori_loop(0, groups, sent, 0)
@@ -390,15 +431,15 @@
         return carry
 
     lax.fori_loop(0, pairs, c_sent, 0)
-    for d in range(1, Y):
-        y_copy(d, False).wait_send()
-        fy_copy(d, False).wait_send()
-    for d in range(Y):
+    for way in range(2):
+        y_half(way).wait_send()
+        y_pair(way).wait_send()
+        f_pair(way, False).wait_send()
+        f_half(way, False).wait_send()
+    for d in range(-1, Y - 1):
         fc_copy(d, False).wait_send()
     z_copy().wait_send()
     fz_copy(False).wait_send()
-    pltpu.make_async_copy(mom, nmom_o, st_sem.at[0]).wait()
-    pltpu.make_async_copy(mast, nmast_o, st_sem.at[1]).wait()
 
 
 def shards(tokens, queries, kv_weight, doc_lengths, local_params, base_copy, master, momentum):
@@ -414,24 +455,24 @@
     outs = pl.pallas_call(
         kernel,
         out_shape=(
-            jax.ShapeDtypeStruct((tok_count, q_width), BF),
-            jax.ShapeDtypeStruct((rows, owned), F32),
-            jax.ShapeDtypeStruct((rows, owned), F32),
-            jax.ShapeDtypeStruct((rows, full), BF),
+            pltpu.VMEM((tok_count, q_width), BF),
+            pltpu.VMEM((rows, owned), F32),
+            pltpu.VMEM((rows, owned), F32),
+            pltpu.VMEM((rows, full), BF),
         ),
         in_specs=[hbm] * 3 + [pl.BlockSpec(memory_space=pltpu.SMEM)] + [hbm] * 4,
-        out_specs=(hbm,) * 4,
+        out_specs=(pl.BlockSpec(memory_space=pltpu.VMEM),) * 4,
         scratch_shapes=[
             pltpu.VMEM((groups, width, 2 * HEAD), BF),
             pltpu.VMEM((tok_count, width), BF),
-            pltpu.VMEM((tok_count, q_width), BF),
             pltpu.VMEM((tok_count, q_width), BF),
             pltpu.VMEM((rows, full), BF),
             pltpu.VMEM((rows, full), BF),
             pltpu.VMEM((pairs, rows, owned), BF),
             pltpu.VMEM((pairs, rows, owned), BF),
             pltpu.VMEM((pairs, rows, owned), BF),
-            pltpu.VMEM((Y - 1, 2, rows, owned), BF),
+            pltpu.VMEM((2, rows, owned), BF),
+            pltpu.VMEM((2, 2, rows, owned), BF),
             pltpu.VMEM((rows, owned), BF),
             pltpu.VMEM((rows, owned), BF),
             pltpu.VMEM((rows, owned), F32),
@@ -439,29 +480,28 @@
             pltpu.VMEM((rows, owned), F32),
             pltpu.VMEM((2, pairs, rows, owned), BF),
             pltpu.VMEM((tok_count, 2 * HEAD), F32),
+            pltpu.VMEM((tok_count, 2 * HEAD), BF),
             pltpu.VMEM((tok_count, tok_count), F32),
             dma((groups, 13)),
             dma((groups, 13)),
             dma((pairs,)),
             dma((pairs,)),
-            dma((Y - 1,)),
-            dma((Y - 1,)),
+            dma((4,)),
+            dma((4,)),
             dma,
             dma,
             dma,
             dma,
-            dma((Y - 1,)),
-            dma((Y - 1,)),
+            dma((4,)),
+            dma((4,)),
             dma((Y,)),
             dma((Y,)),
             dma((groups, 2)),
             dma((6,)),
-            dma((groups,)),
             dma((2, pairs)),
-            dma((2,)),
         ],
         compiler_params=pltpu.CompilerParams(
-            collective_id=0, has_side_effects=True, vmem_limit_bytes=60 * 1024 * 1024
+            collective_id=0, has_side_effects=True, vmem_limit_bytes=48 * 1024 * 1024
         ),
         cost_estimate=pl.CostEstimate(flops=9 * 10**9, bytes_accessed=3 * 10**7, transcendentals=5 * 10**6),
         name="fused",

time: 161 us -> 132 us (0.82); the launches traced: 161 us -> 130 us
  Pallas kernels: 153 us -> 124 us
  local copies, waits for them, and re-layouts: 7.23 us -> 4.82 us
    pallas_call x1, Pallas kernels: 153 us -> 124 us  [shards(): pl.pallas_call(kernel, out_shape=(pltpu.VMEM((tok_count, q_width), BF), p...]
    unnamed x10 -> x4, local copies, waits for them, and re-layouts: 7.23 us -> 4.82 us
where the time goes in v2:
time: 132 us; the launch traced here: 130 us
  Pallas kernels  124 us (94%)
  local copies, waits for them, and re-layouts  4.82 us (4%)
    pallas_call x1, Pallas kernels, shards(): pl.pallas_call(kernel, out_shape=(pltpu.VMEM((tok_count, q_width), BF), p...  124 us
    unnamed x4, local copies, waits for them, and re-layouts  4.82 us

profile of v2, /device:TPU:0, one launch (start us, length us, event | category | flops | bytes accessed | tf_op | source)
XLA Modules:
  0.0 129.8 jit_solution(2538296158557055265)
XLA Ops:
  0.6 124.3 %fused.1 = (bf16[384,4096]{1,0:T(8,128)(2,1)S(1)}, f32[192,512]{1,0:T(8,128)S(1)}, f32[192,512]{1,0:T(8,128)S(1)}, bf16[192,8192]{1,0:T(8,128)(2,1)S(1)}) custom-call(bf16[384,8192]{1,0:T(8,128)(2,1)} %bitcast.7, bf16[384,4096]{1,0:T(8,128)(2,1)} %bitcast.8, bf16[1024,1024]{1,0:T(8,128)(2,1)} %bitcast.10, s32[6]{0:T(128)} %bitcast.11, ...), custom_call_target="tpu_custom_call" | custom-call | flops 8999999488 | bytes 30000000 | tf_op jit(solution)/shard_map/fused/pallas_call | solution.py:455
  124.9 1.7 %copy.16 = bf16[1,384,4096]{2,1,0:T(8,128)(2,1)} copy(bf16[1,384,4096]{2,1,0:T(8,128)(2,1)S(1)} %bitcast.6) | data formatting | bytes 6291456
  126.6 0.7 copy.17
  127.3 0.7 copy.18
  128.1 1.7 %copy.19 = bf16[192,8192]{1,0:T(8,128)(2,1)} copy(bf16[192,8192]{1,0:T(8,128)(2,1)S(1)} %get-tuple-element.15) | data formatting | bytes 6291456

commit v3 on v2

--- a/solution.py
+++ b/solution.py
@@ -15,7 +15,9 @@
 
 X = 4
 Y = 4
-FIRST = 416
+LEAD = 2
+PARTS = 2
+FIRST = 208
 BF = jnp.bfloat16
 F32 = jnp.float32
 
@@ -27,14 +29,16 @@
     kv_send, kv_recv, c_send, c_recv, y_send, y_recv, z_send, z_recv, fz_send, fz_recv, fy_send, fy_recv,
     fc_send, fc_recv, w_sem, in_sem, fo_sem,
 ):
-    groups = wbuf.shape[0]
+    chunks = wbuf.shape[0]
+    groups = chunks // PARTS
     tokens = tok.shape[0]
-    shard = w_h.shape[0]
+    whole = w_h.shape[0]
+    shard = whole // PARTS
     rows, owned = mast.shape
     pairs = csend.shape[0]
     per_group = q.shape[1] // HEAD // groups
     second = shard - FIRST
-    half2 = second // 2
+    half2 = (second // 2 + 15) // 16 * 16
 
     f = lax.axis_index("fsdp")
     r = lax.axis_index("replica")
@@ -59,11 +63,14 @@
     for peer in peers:
         pl.semaphore_signal(barrier, inc=1, device_id=peer, device_id_type=MESH)
 
-    def w_copy(g, side):
+    def w_copy(c, side):
         return pltpu.make_async_copy(
-            w_h.at[:, pl.ds(pl.multiple_of((side * groups + g) * HEAD, HEAD), HEAD)],
-            wbuf.at[g, pl.ds(pl.multiple_of(f * shard, 16), shard), pl.ds(side * HEAD, HEAD)],
-            w_sem.at[g, side],
+            w_h.at[
+                pl.ds(pl.multiple_of(c % PARTS * shard, 16), shard),
+                pl.ds(pl.multiple_of((side * groups + c // PARTS) * HEAD, HEAD), HEAD),
+            ],
+            wbuf.at[c, pl.ds(pl.multiple_of(f * shard, 16), shard), pl.ds(side * HEAD, HEAD)],
+            w_sem.at[c, side],
         )
 
     loads = [
@@ -72,9 +79,9 @@
             ((loc_h, loc), (base_h, base), (tok_h, tok), (q_h, q), (mast_h, mast), (mom_h, mom))
         )
     ]
-    for g in range(groups):
+    for c in range(chunks):
         for side in range(2):
-            w_copy(g, side).start()
+            w_copy(c, side).start()
     for load in loads:
         load.start()
 
@@ -90,7 +97,7 @@
         (place(-1, 0), 0, FIRST, across, place(-1, 1)),
         (place(1, 0), 0, FIRST, across, place(1, 1)),
         (place(-1, 1), FIRST, half2, right, place(2, 1)),
-        (place(1, 1), FIRST + half2, half2, left, place(2, 1)),
+        (place(1, 1), FIRST + half2, second - half2, left, place(2, 1)),
         (place(2, 0), 0, FIRST, across, place(2, 1)),
     )
 
@@ -121,8 +128,8 @@
         send(g, 0, 2, 3, 1)
 
     pl.semaphore_wait(barrier, len(peers))
-    own(0)
-    own(1)
+    for c in range(LEAD):
+        own(c)
 
     ends = []
     total = len_s[0]
@@ -259,15 +266,19 @@
     nq = 3
     qrows = tokens // nq
 
-    def compute(g):
+    def compute(c):
         def part(held):
             return jnp.dot(
-                tok[:, pl.ds(pl.multiple_of(held * shard, shard), shard)],
-                wbuf[g, pl.ds(pl.multiple_of(held * shard, shard), shard), :],
+                tok[:, pl.ds(pl.multiple_of(held * whole + c % PARTS * shard, shard), shard)],
+                wbuf[c, pl.ds(pl.multiple_of(held * shard, shard), shard), :],
                 preferred_element_type=F32,
             )
 
-        acc[...] = part(place(0, 0))
+        @pl.when(c % PARTS == 0)
+        def _():
+            acc[...] = jnp.zeros_like(acc)
+
+        acc[...] += part(place(0, 0))
         acc[...] += part(place(-1, 0))
         acc[...] += part(place(1, 0))
         for held, which in (
@@ -277,10 +288,15 @@
             (place(1, 1), (9,)),
             (place(2, 1), (10, 11, 12)),
         ):
-            arrived(g, *which)
+            arrived(c, *which)
             acc[...] += part(held)
+
+        @pl.when(c % PARTS == PARTS - 1)
+        def _():
+            attend(c // PARTS)
+
+    def attend(g):
         packed[...] = acc[...].astype(BF)
-
         heads = [pl.ds(pl.multiple_of((g * per_group + h) * HEAD, HEAD), HEAD) for h in range(per_group)]
         for i in range(nq):
             at = pl.ds(i * qrows, qrows)
@@ -301,21 +317,7 @@
                 att[at, cols] = jnp.dot(weights, packed[:seen, HEAD:], preferred_element_type=F32).astype(BF)
 
     def turn(t, carry):
-        @pl.when(t == 1)
-        def _():
-            for way in range(2):
-                y_half(way).wait_recv()
-                onward = 2 * ahead(1 - 2 * way) + way
-
-                def body(row):
-                    at = pl.ds(row, tile)
-                    value = ysend[onward, at, :].astype(F32) + yhalf[way, at, :].astype(F32)
-                    ysend[onward, at, :] = value.astype(BF)
-
-                row_tiles(body)
-                y_pair(way).start()
-
-        @pl.when(t < groups)
+        @pl.when(t < chunks)
         def _():
             arrived(t, 0)
             send(t, 4, 5)
@@ -324,7 +326,7 @@
             arrived(t, 3)
             send(t, 7, 9)
 
-        @pl.when(jnp.logical_and(t > 0, t <= groups))
+        @pl.when(jnp.logical_and(t > 0, t <= chunks))
         def _():
             arrived(t - 1, 4)
             send(t - 1, 10)
@@ -333,9 +335,9 @@
             arrived(t - 1, 6)
             send(t - 1, 12)
 
-        @pl.when(t + 2 < groups)
-        def _():
-            own(t + 2)
+        @pl.when(t + LEAD < chunks)
+        def _():
+            own(t + LEAD)
 
         @pl.when(t == 0)
         def _():
@@ -348,6 +350,20 @@
         @pl.when(t == 1)
         def _():
             for way in range(2):
+                y_half(way).wait_recv()
+                onward = 2 * ahead(1 - 2 * way) + way
+
+                def body(row):
+                    at = pl.ds(row, tile)
+                    value = ysend[onward, at, :].astype(F32) + yhalf[way, at, :].astype(F32)
+                    ysend[onward, at, :] = value.astype(BF)
+
+                row_tiles(body)
+                y_pair(way).start()
+
+        @pl.when(t == 2)
+        def _():
+            for way in range(2):
                 y_pair(way).wait_recv()
 
             def body(row):
@@ -357,34 +373,7 @@
             row_tiles(body)
             z_copy().start()
 
-        @pl.when(t == 3)
-        def _():
-            fz_copy(True).wait_recv()
-            for way in range(2):
-                f_pair(way, False).start()
-            fc_copy(0, False).start()
-
-        @pl.when(t == groups + 1)
-        def _():
-            def out_own(j, carry):
-                f_out(core, j).start()
-                return carry
-
-            lax.fori_loop(0, pairs, out_own, 0)
-            for d in range(-1, Y - 1):
-                fc_copy(d, True).wait_recv()
-
-            def out_twin(j, carry):
-                f_out(1 - core, j).start()
-                return carry
-
-            lax.fori_loop(0, pairs, out_twin, 0)
-
-        @pl.when(t > 1)
-        def _():
-            compute(t - 2)
-
-        @pl.when(t == 2)
+        @pl.when(t == 4)
         def _():
             z_copy().wait_recv()
 
@@ -400,29 +389,57 @@
             row_tiles(body)
             fz_copy(False).start()
 
-        @pl.when(t == 3)
+        @pl.when(t == 6)
+        def _():
+            fz_copy(True).wait_recv()
+            for way in range(2):
+                f_pair(way, False).start()
+            fc_copy(0, False).start()
+
+        @pl.when(t == 7)
         def _():
             for way in range(2):
                 f_pair(way, True).wait_recv()
                 f_half(way, False).start()
                 fc_copy(2 * way - 1, False).start()
 
-        @pl.when(t == groups)
+        @pl.when(t == 8)
         def _():
             for way in range(2):
                 f_half(way, True).wait_recv()
             fc_copy(2, False).start()
 
+            def out_own(j, carry):
+                f_out(core, j).start()
+                return carry
+
+            lax.fori_loop(0, pairs, out_own, 0)
+
+        @pl.when(t == chunks + 1)
+        def _():
+            for d in range(-1, Y - 1):
+                fc_copy(d, True).wait_recv()
+
+            def out_twin(j, carry):
+                f_out(1 - core, j).start()
+                return carry
+
+            lax.fori_loop(0, pairs, out_twin, 0)
+
+        @pl.when(t > 1)
+        def _():
+            compute(t - 2)
+
         return carry
 
-    lax.fori_loop(0, groups + 2, turn, 0)
+    lax.fori_loop(0, chunks + 2, turn, 0)
 
     def sent(g, carry):
         for k in range(len(kinds)):
             moved(k, g, False).wait_send()
         return carry
 
-    lax.fori_loop(0, groups, sent, 0)
+    lax.fori_loop(0, chunks, sent, 0)
 
     def c_sent(j, carry):
         c_copy(j).wait_send()
@@ -440,6 +457,17 @@
         fc_copy(d, False).wait_send()
     z_copy().wait_send()
     fz_copy(False).wait_send()
+
+
+def write_out(a, b, c, d, a_o, b_o, c_o, d_o, sem):
+    copies = [
+        pltpu.make_async_copy(src, dst, sem.at[i])
+        for i, (src, dst) in enumerate(((a, a_o), (d, d_o), (b, b_o), (c, c_o)))
+    ]
+    for copy in copies:
+        copy.start()
+    for copy in copies:
+        copy.wait()
 
 
 def shards(tokens, queries, kv_weight, doc_lengths, local_params, base_copy, master, momentum):
@@ -463,7 +491,7 @@
         in_specs=[hbm] * 3 + [pl.BlockSpec(memory_space=pltpu.SMEM)] + [hbm] * 4,
         out_specs=(pl.BlockSpec(memory_space=pltpu.VMEM),) * 4,
         scratch_shapes=[
-            pltpu.VMEM((groups, width, 2 * HEAD), BF),
+            pltpu.VMEM((groups * PARTS, width // PARTS, 2 * HEAD), BF),
             pltpu.VMEM((tok_count, width), BF),
             pltpu.VMEM((tok_count, q_width), BF),
             pltpu.VMEM((rows, full), BF),
@@ -482,8 +510,8 @@
             pltpu.VMEM((tok_count, 2 * HEAD), F32),
             pltpu.VMEM((tok_count, 2 * HEAD), BF),
             pltpu.VMEM((tok_count, tok_count), F32),
-            dma((groups, 13)),
-            dma((groups, 13)),
+            dma((groups * PARTS, 13)),
+            dma((groups * PARTS, 13)),
             dma((pairs,)),
             dma((pairs,)),
             dma((4,)),
@@ -496,7 +524,7 @@
             dma((4,)),
             dma((Y,)),
             dma((Y,)),
-            dma((groups, 2)),
+            dma((groups * PARTS, 2)),
             dma((6,)),
             dma((2, pairs)),
         ],
@@ -508,7 +536,15 @@
     )(
         tokens[0], queries[0], kv_weight[0], doc_lengths[0, 0], local_params[0], base_copy, master, momentum
     )
-    attended, new_master, new_momentum, fresh = outs
+    attended, new_master, new_momentum, fresh = pl.pallas_call(
+        write_out,
+        out_shape=tuple(jax.ShapeDtypeStruct(o.shape, o.dtype) for o in outs),
+        in_specs=[pl.BlockSpec(memory_space=pltpu.VMEM)] * 4,
+        out_specs=(hbm,) * 4,
+        scratch_shapes=[dma((4,))],
+        compiler_params=pltpu.CompilerParams(vmem_limit_bytes=2 * 1024 * 1024),
+        name="write_out",
+    )(*outs)
     return attended[None], new_master, new_momentum, fresh
 
 

time: 132 us -> 127 us (0.962); the launches traced: 130 us -> 127 us
  local copies, waits for them, and re-layouts: 4.82 us -> 0 us
  Pallas kernels: 124 us -> 126 us
    unnamed x4 -> x0, local copies, waits for them, and re-layouts: 4.82 us -> none
    pallas_call x0 -> x1, Pallas kernels: none -> 2.97 us  [shards(): pl.pallas_call(write_out, out_shape=tuple((jax.ShapeDtypeStruct(o.shape,...]
where the time goes in v3:
time: 127 us
  Pallas kernels  126 us (99%)
    pallas_call x1, Pallas kernels, shards(): pl.pallas_call(kernel, out_shape=(pltpu.VMEM((tok_count, q_width), BF), p...  123 us
    pallas_call x1, Pallas kernels, shards(): pl.pallas_call(write_out, out_shape=tuple((jax.ShapeDtypeStruct(o.shape,...  2.97 us

profile of v3, /device:TPU:0, one launch (start us, length us, event | category | flops | bytes accessed | tf_op | source)
XLA Modules:
  0.0 126.9 jit_solution(11835258653505022619)
XLA Ops:
  0.6 123.3 %fused.1 = (bf16[384,4096]{1,0:T(8,128)(2,1)S(1)}, f32[192,512]{1,0:T(8,128)S(1)}, f32[192,512]{1,0:T(8,128)S(1)}, bf16[192,8192]{1,0:T(8,128)(2,1)S(1)}) custom-call(bf16[384,8192]{1,0:T(8,128)(2,1)} %bitcast.6, bf16[384,4096]{1,0:T(8,128)(2,1)} %bitcast.7, bf16[1024,1024]{1,0:T(8,128)(2,1)} %bitcast.10, s32[6]{0:T(128)} %bitcast.11, ...), custom_call_target="tpu_custom_call" | custom-call | flops 8999999488 | bytes 30000000 | tf_op jit(solution)/shard_map/fused/pallas_call | solution.py:483
  123.9 3.0 %write_out.1 = (bf16[384,4096]{1,0:T(8,128)(2,1)}, f32[192,512]{1,0:T(8,128)}, f32[192,512]{1,0:T(8,128)}, bf16[192,8192]{1,0:T(8,128)(2,1)}) custom-call(bf16[384,4096]{1,0:T(8,128)(2,1)S(1)} %get-tuple-element.12.a, f32[192,512]{1,0:T(8,128)S(1)} %get-tuple-element.13.b, f32[192,512]{1,0:T(8,128)S(1)} %get-tuple-element.14.c, ...), custom_call_target="tpu_custom_call" | custom-call | tf_op jit(solution)/shard_map/write_out/pallas_call | solution.py:539

commit v4 on v3

--- a/solution.py
+++ b/solution.py
@@ -17,7 +17,6 @@
 Y = 4
 LEAD = 2
 PARTS = 2
-FIRST = 208
 BF = jnp.bfloat16
 F32 = jnp.float32
 
@@ -25,8 +24,8 @@
 def kernel(
     tok_h, q_h, w_h, len_s, loc_h, base_h, mast_h, mom_h,
     att, mast_o, mom_o, fresh_o,
-    wbuf, tok, q, loc, base, csend, crecv, ysend, yhalf, yrecv, zsend, zrecv, zown, mast, mom, fbuf, acc, packed, bias,
-    kv_send, kv_recv, c_send, c_recv, y_send, y_recv, z_send, z_recv, fz_send, fz_recv, fy_send, fy_recv,
+    wbuf, tok, q, loc, base, csend, crecv, ysend, yhalf, yrecv, zsend, zrecv, zown, mast, mom, fbuf, acc, given, gained, theirs, packed, bias,
+    kv_send, kv_recv, tok_send, tok_recv, g_send, g_recv, c_send, c_recv, y_send, y_recv, z_send, z_recv, fz_send, fz_recv, fy_send, fy_recv,
     fc_send, fc_recv, w_sem, in_sem, fo_sem,
 ):
     chunks = wbuf.shape[0]
@@ -37,8 +36,8 @@
     rows, owned = mast.shape
     pairs = csend.shape[0]
     per_group = q.shape[1] // HEAD // groups
-    second = shard - FIRST
-    half2 = (second // 2 + 15) // 16 * 16
+    half = shard // 2
+    quarter = shard // 4
 
     f = lax.axis_index("fsdp")
     r = lax.axis_index("replica")
@@ -66,8 +65,8 @@
     def w_copy(c, side):
         return pltpu.make_async_copy(
             w_h.at[
-                pl.ds(pl.multiple_of(c % PARTS * shard, 16), shard),
-                pl.ds(pl.multiple_of((side * groups + c // PARTS) * HEAD, HEAD), HEAD),
+                pl.ds(pl.multiple_of(c // groups * shard, 16), shard),
+                pl.ds(pl.multiple_of((side * groups + c % groups) * HEAD, HEAD), HEAD),
             ],
             wbuf.at[c, pl.ds(pl.multiple_of(f * shard, 16), shard), pl.ds(side * HEAD, HEAD)],
             w_sem.at[c, side],
@@ -86,20 +85,30 @@
         load.start()
 
     kinds = (
-        (place(0, 0), FIRST, second, across, place(0, 1)),
-        (place(0, 0), 0, FIRST, across, place(0, 1)),
+        (place(0, 0), half, half, across, place(0, 1)),
         (place(0, 0), 0, shard, right, place(-1, 0)),
         (place(0, 0), 0, shard, left, place(1, 0)),
-        (place(0, 1), FIRST, second, right, place(-1, 1)),
-        (place(0, 1), FIRST, second, left, place(1, 1)),
-        (place(-1, 0), 0, shard // 2, right, place(2, 0)),
-        (place(1, 0), shard // 2, shard // 2, left, place(2, 0)),
-        (place(-1, 0), 0, FIRST, across, place(-1, 1)),
-        (place(1, 0), 0, FIRST, across, place(1, 1)),
-        (place(-1, 1), FIRST, half2, right, place(2, 1)),
-        (place(1, 1), FIRST + half2, second - half2, left, place(2, 1)),
-        (place(2, 0), 0, FIRST, across, place(2, 1)),
+        (place(0, 1), half, half, right, place(-1, 1)),
+        (place(0, 1), half, half, left, place(1, 1)),
+        (place(-1, 0), 0, half, right, place(2, 0)),
+        (place(1, 0), half, half, left, place(2, 0)),
+        (place(-1, 1), half, quarter, right, place(2, 1)),
+        (place(1, 1), half + quarter, quarter, left, place(2, 1)),
     )
+
+    def tok_copy(h, xx, arriving):
+        cols = pl.ds(pl.multiple_of((xx * 2 + 1 - z) * whole + h * shard, half), half)
+        there = theirs.at[:, pl.ds((h * X + xx) * half, half)]
+        return pltpu.make_async_remote_copy(
+            src_ref=there if arriving else tok.at[:, cols], dst_ref=there, send_sem=tok_send.at[h, xx],
+            recv_sem=tok_recv.at[h, xx], device_id=across, device_id_type=MESH,
+        )
+
+    def sums_back(g):
+        return pltpu.make_async_remote_copy(
+            src_ref=given.at[g], dst_ref=gained.at[g], send_sem=g_send.at[g], recv_sem=g_recv.at[g],
+            device_id=across, device_id_type=MESH,
+        )
 
     def moved(k, g, arriving):
         source, start, count, target, other = kinds[k]
@@ -125,11 +134,17 @@
     def own(g):
         w_copy(g, 0).wait()
         w_copy(g, 1).wait()
-        send(g, 0, 2, 3, 1)
+        send(g, 0, 1, 2)
 
     pl.semaphore_wait(barrier, len(peers))
     for c in range(LEAD):
         own(c)
+
+    loads[2].wait()
+    for xx in range(X):
+        tok_copy(0, xx, False).start()
+    given[...] = jnp.zeros_like(given)
+    acc[...] = jnp.zeros_like(acc)
 
     ends = []
     total = len_s[0]
@@ -266,37 +281,42 @@
     nq = 3
     qrows = tokens // nq
 
+    def product(tokens_of, first, c, row, count):
+        return jnp.dot(
+            tokens_of[:, pl.ds(pl.multiple_of(first, half), count)],
+            wbuf[c, pl.ds(pl.multiple_of(row, half), count), :],
+            preferred_element_type=F32,
+        )
+
+    def give(c):
+        g, h = c % groups, c // groups
+        for xx in range(X):
+            given[g] += product(theirs, (h * X + xx) * half, c, (xx * 2 + z) * shard, half)
+
     def compute(c):
-        def part(held):
-            return jnp.dot(
-                tok[:, pl.ds(pl.multiple_of(held * whole + c % PARTS * shard, shard), shard)],
-                wbuf[c, pl.ds(pl.multiple_of(held * shard, shard), shard), :],
-                preferred_element_type=F32,
-            )
-
-        @pl.when(c % PARTS == 0)
-        def _():
-            acc[...] = jnp.zeros_like(acc)
-
-        acc[...] += part(place(0, 0))
-        acc[...] += part(place(-1, 0))
-        acc[...] += part(place(1, 0))
-        for held, which in (
-            (place(0, 1), (1,)),
-            (place(2, 0), (7,)),
-            (place(-1, 1), (8,)),
-            (place(1, 1), (9,)),
-            (place(2, 1), (10, 11, 12)),
-        ):
-            arrived(c, *which)
-            acc[...] += part(held)
-
-        @pl.when(c % PARTS == PARTS - 1)
-        def _():
-            attend(c // PARTS)
+        g, h = c % groups, c // groups
+
+        def add(held, start, count):
+            acc[g] += product(tok, held * whole + h * shard + start, c, held * shard + start, count)
+
+        add(place(0, 0), 0, shard)
+        add(place(-1, 0), 0, shard)
+        add(place(1, 0), 0, shard)
+        add(place(0, 1), half, half)
+        add(place(-1, 1), half, half)
+        add(place(1, 1), half, half)
+        arrived(c, 6)
+        add(place(2, 0), 0, shard)
+        arrived(c, 7, 8)
+        add(place(2, 1), half, half)
+
+        @pl.when(h == PARTS - 1)
+        def _():
+            sums_back(g).wait_recv()
+            attend(g)
 
     def attend(g):
-        packed[...] = acc[...].astype(BF)
+        packed[...] = (acc[g] + gained[g]).astype(BF)
         heads = [pl.ds(pl.multiple_of((g * per_group + h) * HEAD, HEAD), HEAD) for h in range(per_group)]
         for i in range(nq):
             at = pl.ds(i * qrows, qrows)
@@ -319,32 +339,62 @@
     def turn(t, carry):
         @pl.when(t < chunks)
         def _():
-            arrived(t, 0)
-            send(t, 4, 5)
+            arrived(t, 1)
+            send(t, 5)
             arrived(t, 2)
-            send(t, 6, 8)
-            arrived(t, 3)
-            send(t, 7, 9)
+            send(t, 6)
+
+        @pl.when(t + LEAD < chunks)
+        def _():
+            own(t + LEAD)
+
+        @pl.when(t == 1)
+        def _():
+            for xx in range(X // 2):
+                tok_copy(1, xx, False).start()
+
+        @pl.when(t == 2)
+        def _():
+            for xx in range(X // 2, X):
+                tok_copy(1, xx, False).start()
+
+        @pl.when(t == 1)
+        def _():
+            for xx in range(X):
+                tok_copy(0, xx, True).wait_recv()
+
+        @pl.when(t == groups + 1)
+        def _():
+            for xx in range(X):
+                tok_copy(1, xx, True).wait_recv()
+
+        @pl.when(jnp.logical_and(t > 1, t <= chunks + 1))
+        def _():
+            arrived(t - 2, 0)
+            send(t - 2, 3, 4)
 
         @pl.when(jnp.logical_and(t > 0, t <= chunks))
         def _():
-            arrived(t - 1, 4)
-            send(t - 1, 10)
             arrived(t - 1, 5)
-            send(t - 1, 11)
-            arrived(t - 1, 6)
-            send(t - 1, 12)
-
-        @pl.when(t + LEAD < chunks)
-        def _():
-            own(t + LEAD)
+            give(t - 1)
+
+        @pl.when(jnp.logical_and(t > groups, t <= chunks))
+        def _():
+            sums_back(t - 1 - groups).start()
+
+        @pl.when(jnp.logical_and(t > 2, t <= chunks + 2))
+        def _():
+            arrived(t - 3, 3)
+            send(t - 3, 7)
+            arrived(t - 3, 4)
+            send(t - 3, 8)
 
         @pl.when(t == 0)
         def _():
             lax.fori_loop(0, pairs, with_twin, 0)
             for way in range(2):
                 y_half(way).start()
-            for load in loads[2:]:
+            for load in loads[3:]:
                 load.wait()
 
         @pl.when(t == 1)
@@ -415,7 +465,7 @@
 
             lax.fori_loop(0, pairs, out_own, 0)
 
-        @pl.when(t == chunks + 1)
+        @pl.when(t == chunks + 2)
         def _():
             for d in range(-1, Y - 1):
                 fc_copy(d, True).wait_recv()
@@ -426,13 +476,13 @@
 
             lax.fori_loop(0, pairs, out_twin, 0)
 
-        @pl.when(t > 1)
-        def _():
-            compute(t - 2)
+        @pl.when(t > 3)
+        def _():
+            compute(t - 4)
 
         return carry
 
-    lax.fori_loop(0, chunks + 2, turn, 0)
+    lax.fori_loop(0, chunks + 4, turn, 0)
 
     def sent(g, carry):
         for k in range(len(kinds)):
@@ -440,6 +490,11 @@
         return carry
 
     lax.fori_loop(0, chunks, sent, 0)
+    for h in range(PARTS):
+        for xx in range(X):
+            tok_copy(h, xx, False).wait_send()
+    for g in range(groups):
+        sums_back(g).wait_send()
 
     def c_sent(j, carry):
         c_copy(j).wait_send()
@@ -507,11 +562,18 @@
             pltpu.VMEM((rows, owned), F32),
             pltpu.VMEM((rows, owned), F32),
             pltpu.VMEM((2, pairs, rows, owned), BF),
-            pltpu.VMEM((tok_count, 2 * HEAD), F32),
+            pltpu.VMEM((groups, tok_count, 2 * HEAD), F32),
+            pltpu.VMEM((groups, tok_count, 2 * HEAD), F32),
+            pltpu.VMEM((groups, tok_count, 2 * HEAD), F32),
+            pltpu.VMEM((tok_count, width // 4), BF),
             pltpu.VMEM((tok_count, 2 * HEAD), BF),
             pltpu.VMEM((tok_count, tok_count), F32),
-            dma((groups * PARTS, 13)),
-            dma((groups * PARTS, 13)),
+            dma((groups * PARTS, 9)),
+            dma((groups * PARTS, 9)),
+            dma((PARTS, X)),
+            dma((PARTS, X)),
+            dma((groups,)),
+            dma((groups,)),
             dma((pairs,)),
             dma((pairs,)),
             dma((4,)),
@@ -529,7 +591,7 @@
             dma((2, pairs)),
         ],
         compiler_params=pltpu.CompilerParams(
-            collective_id=0, has_side_effects=True, vmem_limit_bytes=48 * 1024 * 1024
+            collective_id=0, has_side_effects=True, vmem_limit_bytes=51 * 1024 * 1024
         ),
         cost_estimate=pl.CostEstimate(flops=9 * 10**9, bytes_accessed=3 * 10**7, transcendentals=5 * 10**6),
         name="fused",

time: 127 us -> 122 us (0.961)
  Pallas kernels: 126 us -> 121 us
    pallas_call x1, Pallas kernels: 123 us -> 118 us  [shards(): pl.pallas_call(kernel, out_shape=(pltpu.VMEM((tok_count, q_width), BF), p...]
where the time goes in v4:
time: 122 us; the launch traced here: 121 us
  Pallas kernels  121 us (99%)
    pallas_call x1, Pallas kernels, shards(): pl.pallas_call(kernel, out_shape=(pltpu.VMEM((tok_count, q_width), BF), p...  118 us
    pallas_call x1, Pallas kernels, shards(): pl.pallas_call(write_out, out_shape=tuple((jax.ShapeDtypeStruct(o.shape,...  2.97 us

profile of v4, /device:TPU:0, one launch (start us, length us, event | category | flops | bytes accessed | tf_op | source)
XLA Modules:
  0.0 121.5 jit_solution(5699171706056815256)
XLA Ops:
  0.6 117.9 %fused.1 = (bf16[384,4096]{1,0:T(8,128)(2,1)S(1)}, f32[192,512]{1,0:T(8,128)S(1)}, f32[192,512]{1,0:T(8,128)S(1)}, bf16[192,8192]{1,0:T(8,128)(2,1)S(1)}) custom-call(bf16[384,8192]{1,0:T(8,128)(2,1)} %bitcast.6, bf16[384,4096]{1,0:T(8,128)(2,1)} %bitcast.7, bf16[1024,1024]{1,0:T(8,128)(2,1)} %bitcast.10, s32[6]{0:T(128)} %bitcast.11, ...), custom_call_target="tpu_custom_call" | custom-call | flops 8999999488 | bytes 30000000 | tf_op jit(solution)/shard_map/fused/pallas_call | solution.py:538
  118.5 3.0 %write_out.1 = (bf16[384,4096]{1,0:T(8,128)(2,1)}, f32[192,512]{1,0:T(8,128)}, f32[192,512]{1,0:T(8,128)}, bf16[192,8192]{1,0:T(8,128)(2,1)}) custom-call(bf16[384,4096]{1,0:T(8,128)(2,1)S(1)} %get-tuple-element.12.a, f32[192,512]{1,0:T(8,128)S(1)} %get-tuple-element.13.b, f32[192,512]{1,0:T(8,128)S(1)} %get-tuple-element.14.c, ...), custom_call_target="tpu_custom_call" | custom-call | tf_op jit(solution)/shard_map/write_out/pallas_call | solution.py:601

commit v5 on v4

--- a/solution.py
+++ b/solution.py
@@ -21,10 +21,33 @@
 F32 = jnp.float32
 
 
+def attend(q, q_first, packed, bias, att, att_first, heads):
+    tokens = q.shape[0]
+    nq = 3
+    qrows = tokens // nq
+    from_cols = [pl.ds(pl.multiple_of(q_first + h * HEAD, HEAD), HEAD) for h in range(heads)]
+    to_cols = [pl.ds(pl.multiple_of(att_first + h * HEAD, HEAD), HEAD) for h in range(heads)]
+    for i in range(nq):
+        at = pl.ds(i * qrows, qrows)
+        seen = (i + 1) * qrows
+        scores = [
+            lax.dot_general(q[at, cols], packed[:seen, :HEAD], (((1,), (1,)), ((), ())), preferred_element_type=F32)
+            * (HEAD**-0.5 * LOG2E)
+            + bias[at, :seen]
+            for cols in from_cols
+        ]
+        highest = [jnp.max(s, axis=1, keepdims=True) for s in scores]
+        expo = [jnp.exp2(s - m) for s, m in zip(scores, highest)]
+        over = [1.0 / jnp.sum(e, axis=1, keepdims=True) for e in expo]
+        for cols, e, o in zip(to_cols, expo, over):
+            weights = (e * o).astype(BF)
+            att[at, cols] = jnp.dot(weights, packed[:seen, HEAD:], preferred_element_type=F32).astype(BF)
+
+
 def kernel(
     tok_h, q_h, w_h, len_s, loc_h, base_h, mast_h, mom_h,
-    att, mast_o, mom_o, fresh_o,
-    wbuf, tok, q, loc, base, csend, crecv, ysend, yhalf, yrecv, zsend, zrecv, zown, mast, mom, fbuf, acc, given, gained, theirs, packed, bias,
+    att, mast_o, mom_o, fresh_o, packed, bias,
+    wbuf, tok, q, loc, base, csend, crecv, ysend, yhalf, yrecv, zsend, zrecv, zown, mast, mom, fbuf, acc, given, gained, theirs,
     kv_send, kv_recv, tok_send, tok_recv, g_send, g_recv, c_send, c_recv, y_send, y_recv, z_send, z_recv, fz_send, fz_recv, fy_send, fy_recv,
     fc_send, fc_recv, w_sem, in_sem, fo_sem,
 ):
@@ -278,9 +301,6 @@
 
         lax.fori_loop(0, rows // tile, step, 0)
 
-    nq = 3
-    qrows = tokens // nq
-
     def product(tokens_of, first, c, row, count):
         return jnp.dot(
             tokens_of[:, pl.ds(pl.multiple_of(first, half), count)],
@@ -293,48 +313,41 @@
         for xx in range(X):
             given[g] += product(theirs, (h * X + xx) * half, c, (xx * 2 + z) * shard, half)
 
-    def compute(c):
+    def adder(c):
         g, h = c % groups, c // groups
 
         def add(held, start, count):
             acc[g] += product(tok, held * whole + h * shard + start, c, held * shard + start, count)
 
+        return add
+
+    def keep(c):
+        add = adder(c)
         add(place(0, 0), 0, shard)
         add(place(-1, 0), 0, shard)
         add(place(1, 0), 0, shard)
+        arrived(c, 6)
+        add(place(2, 0), 0, shard)
+
+    def compute(c):
+        g, h = c % groups, c // groups
+        add = adder(c)
         add(place(0, 1), half, half)
         add(place(-1, 1), half, half)
         add(place(1, 1), half, half)
-        arrived(c, 6)
-        add(place(2, 0), 0, shard)
         arrived(c, 7, 8)
         add(place(2, 1), half, half)
 
         @pl.when(h == PARTS - 1)
         def _():
             sums_back(g).wait_recv()
-            attend(g)
-
-    def attend(g):
-        packed[...] = (acc[g] + gained[g]).astype(BF)
-        heads = [pl.ds(pl.multiple_of((g * per_group + h) * HEAD, HEAD), HEAD) for h in range(per_group)]
-        for i in range(nq):
-            at = pl.ds(i * qrows, qrows)
-            seen = (i + 1) * qrows
-            scores = [
-                lax.dot_general(
-                    q[at, cols], packed[:seen, :HEAD], (((1,), (1,)), ((), ())), preferred_element_type=F32
-                )
-                * (HEAD**-0.5 * LOG2E)
-                + bias[at, :seen]
-                for cols in heads
-            ]
-            highest = [jnp.max(s, axis=1, keepdims=True) for s in scores]
-            expo = [jnp.exp2(s - m) for s, m in zip(scores, highest)]
-            over = [1.0 / jnp.sum(e, axis=1, keepdims=True) for e in expo]
-            for cols, e, o in zip(heads, expo, over):
-                weights = (e * o).astype(BF)
-                att[at, cols] = jnp.dot(weights, packed[:seen, HEAD:], preferred_element_type=F32).astype(BF)
+            packed[...] = (acc[g] + gained[g]).astype(BF)
+
+            @pl.when(g < groups - 1)
+            def _():
+                first = pl.multiple_of(g * per_group * HEAD, HEAD)
+                attend(q, first, packed, bias, att, first, per_group)
+
 
     def turn(t, carry):
         @pl.when(t < chunks)
@@ -388,6 +401,10 @@
             send(t - 3, 7)
             arrived(t - 3, 4)
             send(t - 3, 8)
+
+        @pl.when(jnp.logical_and(t > 0, t <= chunks))
+        def _():
+            keep(t - 1)
 
         @pl.when(t == 0)
         def _():
@@ -514,13 +531,19 @@
     fz_copy(False).wait_send()
 
 
-def write_out(a, b, c, d, a_o, b_o, c_o, d_o, sem):
-    copies = [
-        pltpu.make_async_copy(src, dst, sem.at[i])
-        for i, (src, dst) in enumerate(((a, a_o), (d, d_o), (b, b_o), (c, c_o)))
-    ]
+def write_out(q_h, att, mast, mom, fresh, packed, bias, att_o, mast_o, mom_o, fresh_o, q, last, sem):
+    done = att.shape[1]
+    more = last.shape[1]
+    load = pltpu.make_async_copy(q_h.at[:, pl.ds(done, more)], q, sem.at[0])
+    load.start()
+    pairs = ((att, att_o.at[:, pl.ds(0, done)]), (fresh, fresh_o), (mast, mast_o), (mom, mom_o))
+    copies = [pltpu.make_async_copy(src, dst, sem.at[i + 1]) for i, (src, dst) in enumerate(pairs)]
     for copy in copies:
         copy.start()
+    load.wait()
+    attend(q, 0, packed, bias, last, 0, more // HEAD)
+    copies.append(pltpu.make_async_copy(last, att_o.at[:, pl.ds(done, more)], sem.at[len(pairs) + 1]))
+    copies[-1].start()
     for copy in copies:
         copy.wait()
 
@@ -538,13 +561,15 @@
     outs = pl.pallas_call(
         kernel,
         out_shape=(
-            pltpu.VMEM((tok_count, q_width), BF),
+            pltpu.VMEM((tok_count, q_width - q_width // groups), BF),
             pltpu.VMEM((rows, owned), F32),
             pltpu.VMEM((rows, owned), F32),
             pltpu.VMEM((rows, full), BF),
+            pltpu.VMEM((tok_count, 2 * HEAD), BF),
+            pltpu.VMEM((tok_count, tok_count), F32),
         ),
         in_specs=[hbm] * 3 + [pl.BlockSpec(memory_space=pltpu.SMEM)] + [hbm] * 4,
-        out_specs=(pl.BlockSpec(memory_space=pltpu.VMEM),) * 4,
+        out_specs=(pl.BlockSpec(memory_space=pltpu.VMEM),) * 6,
         scratch_shapes=[
             pltpu.VMEM((groups * PARTS, width // PARTS, 2 * HEAD), BF),
             pltpu.VMEM((tok_count, width), BF),
@@ -566,8 +591,6 @@
             pltpu.VMEM((groups, tok_count, 2 * HEAD), F32),
             pltpu.VMEM((groups, tok_count, 2 * HEAD), F32),
             pltpu.VMEM((tok_count, width // 4), BF),
-            pltpu.VMEM((tok_count, 2 * HEAD), BF),
-            pltpu.VMEM((tok_count, tok_count), F32),
             dma((groups * PARTS, 9)),
             dma((groups * PARTS, 9)),
             dma((PARTS, X)),
@@ -600,13 +623,22 @@
     )
     attended, new_master, new_momentum, fresh = pl.pallas_call(
         write_out,
-        out_shape=tuple(jax.ShapeDtypeStruct(o.shape, o.dtype) for o in outs),
-        in_specs=[pl.BlockSpec(memory_space=pltpu.VMEM)] * 4,
+        out_shape=(
+            jax.ShapeDtypeStruct((tok_count, q_width), BF),
+            jax.ShapeDtypeStruct((rows, owned), F32),
+            jax.ShapeDtypeStruct((rows, owned), F32),
+            jax.ShapeDtypeStruct((rows, full), BF),
+        ),
+        in_specs=[hbm] + [pl.BlockSpec(memory_space=pltpu.VMEM)] * 6,
         out_specs=(hbm,) * 4,
-        scratch_shapes=[dma((4,))],
-        compiler_params=pltpu.CompilerParams(vmem_limit_bytes=2 * 1024 * 1024),
+        scratch_shapes=[
+            pltpu.VMEM((tok_count, q_width // groups), BF),
+            pltpu.VMEM((tok_count, q_width // groups), BF),
+            dma((6,)),
+        ],
+        compiler_params=pltpu.CompilerParams(vmem_limit_bytes=12 * 1024 * 1024),
         name="write_out",
-    )(*outs)
+    )(queries[0], *outs)
     return attended[None], new_master, new_momentum, fresh
 
 

time: 122 us -> 119 us (0.975)
  Pallas kernels: 121 us -> 118 us
    pallas_call x2, Pallas kernels: 121 us -> 118 us  [the longest x1 115 us: shards(): pl.pallas_call(kernel, out_shape=(pltpu.VMEM((tok_count, q_width - q_widt...]
where the time goes in v5:
time: 119 us
  Pallas kernels  118 us (99%)
    pallas_call x1, Pallas kernels, shards(): pl.pallas_call(kernel, out_shape=(pltpu.VMEM((tok_count, q_width - q_widt...  115 us
    pallas_call x1, Pallas kernels, shards(): pl.pallas_call(write_out, out_shape=(jax.ShapeDtypeStruct((tok_count, q_w...  3.05 us

profile of v5, /device:TPU:0, one launch (start us, length us, event | category | flops | bytes accessed | tf_op | source)
XLA Modules:
  0.0 118.8 jit_solution(10906608944812491255)
XLA Ops:
  0.6 0.0 copy-start
  0.6 115.1 %fused.1 = (bf16[384,3072]{1,0:T(8,128)(2,1)S(1)}, f32[192,512]{1,0:T(8,128)S(1)}, f32[192,512]{1,0:T(8,128)S(1)}, bf16[192,8192]{1,0:T(8,128)(2,1)S(1)}, bf16[3...) custom-call(bf16[384,8192]{1,0:T(8,128)(2,1)} %bitcast.8, bf16[384,4096]{1,0:T(8,128)(2,1)} %bitcast.6, ...), custom_call_target="tpu_custom_call" | custom-call | flops 8999999488 | bytes 30000000 | tf_op jit(solution)/shard_map/fused/pallas_call | solution.py:561
  115.7 0.0 copy-done
  115.7 3.1 %write_out.1 = (bf16[384,4096]{1,0:T(8,128)(2,1)}, f32[192,512]{1,0:T(8,128)}, f32[192,512]{1,0:T(8,128)}, bf16[192,8192]{1,0:T(8,128)(2,1)}) custom-call(bf16[384,4096]{1,0:T(8,128)(2,1)S(1)} %bitcast.7, bf16[384,3072]{1,0:T(8,128)(2,1)S(1)} %get-tuple-element.14.att, f32[192,512]{1,0:T(8,128)S(1)} %get-tuple-element.15.mast, ...), custom_call_target="tpu_custom_call" | custom-call | tf_op jit(solution)/shard_map/write_out/pallas_call | solution.py:624
Async XLA Ops:
  0.6 115.1 %copy-start = (bf16[1,384,4096]{2,1,0:T(8,128)(2,1)S(1)}, bf16[1,384,4096]{2,1,0:T(8,128)(2,1)}, u32[]{:S(2)}) copy-start(bf16[1,384,4096]{2,1,0:T(8,128)(2,1)} %param.9) | copy-start | bytes 9437188

commit v6 on v5

--- a/solution.py
+++ b/solution.py
@@ -17,6 +17,7 @@
 Y = 4
 LEAD = 2
 PARTS = 2
+LATE = 16
 BF = jnp.bfloat16
 F32 = jnp.float32
 
@@ -60,7 +61,7 @@
     pairs = csend.shape[0]
     per_group = q.shape[1] // HEAD // groups
     half = shard // 2
-    quarter = shard // 4
+    up = ((half - LATE) // 2 + 15) // 16 * 16
 
     f = lax.axis_index("fsdp")
     r = lax.axis_index("replica")
@@ -111,12 +112,15 @@
         (place(0, 0), half, half, across, place(0, 1)),
         (place(0, 0), 0, shard, right, place(-1, 0)),
         (place(0, 0), 0, shard, left, place(1, 0)),
-        (place(0, 1), half, half, right, place(-1, 1)),
-        (place(0, 1), half, half, left, place(1, 1)),
+        (place(0, 1), half + LATE, half - LATE, right, place(-1, 1)),
+        (place(0, 1), half + LATE, half - LATE, left, place(1, 1)),
         (place(-1, 0), 0, half, right, place(2, 0)),
         (place(1, 0), half, half, left, place(2, 0)),
-        (place(-1, 1), half, quarter, right, place(2, 1)),
-        (place(1, 1), half + quarter, quarter, left, place(2, 1)),
+        (place(-1, 1), half + LATE, up, right, place(2, 1)),
+        (place(1, 1), half + LATE + up, half - LATE - up, left, place(2, 1)),
+        (place(-1, 0), half, LATE, across, place(-1, 1)),
+        (place(1, 0), half, LATE, across, place(1, 1)),
+        (place(2, 0), half, LATE, across, place(2, 1)),
     )
 
     def tok_copy(h, xx, arriving):
@@ -327,15 +331,17 @@
         add(place(-1, 0), 0, shard)
         add(place(1, 0), 0, shard)
         arrived(c, 6)
+        send(c, 11)
         add(place(2, 0), 0, shard)
 
     def compute(c):
         g, h = c % groups, c // groups
         add = adder(c)
         add(place(0, 1), half, half)
+        arrived(c, 9, 10)
         add(place(-1, 1), half, half)
         add(place(1, 1), half, half)
-        arrived(c, 7, 8)
+        arrived(c, 7, 8, 11)
         add(place(2, 1), half, half)
 
         @pl.when(h == PARTS - 1)
@@ -353,9 +359,9 @@
         @pl.when(t < chunks)
         def _():
             arrived(t, 1)
-            send(t, 5)
+            send(t, 5, 9)
             arrived(t, 2)
-            send(t, 6)
+            send(t, 6, 10)
 
         @pl.when(t + LEAD < chunks)
         def _():
@@ -493,6 +499,42 @@
 
             lax.fori_loop(0, pairs, out_twin, 0)
 
+        @pl.when(t > 4)
+        def _():
+            for k in range(len(kinds)):
+                moved(k, t - 5, False).wait_send()
+
+        @pl.when(t == chunks + 1)
+        def _():
+            def c_sent(j, carry):
+                c_copy(j).wait_send()
+                return carry
+
+            lax.fori_loop(0, pairs, c_sent, 0)
+            for way in range(2):
+                y_half(way).wait_send()
+                y_pair(way).wait_send()
+                f_pair(way, False).wait_send()
+                f_half(way, False).wait_send()
+            for d in range(-1, Y - 1):
+                fc_copy(d, False).wait_send()
+            z_copy().wait_send()
+            fz_copy(False).wait_send()
+            for h in range(PARTS):
+                for xx in range(X):
+                    tok_copy(h, xx, False).wait_send()
+            for g in range(groups - 1):
+                sums_back(g).wait_send()
+
+        @pl.when(t == chunks + 3)
+        def _():
+            def written(j, carry):
+                f_out(0, j).wait()
+                f_out(1, j).wait()
+                return carry
+
+            lax.fori_loop(0, pairs, written, 0)
+
         @pl.when(t > 3)
         def _():
             compute(t - 4)
@@ -501,34 +543,9 @@
 
     lax.fori_loop(0, chunks + 4, turn, 0)
 
-    def sent(g, carry):
-        for k in range(len(kinds)):
-            moved(k, g, False).wait_send()
-        return carry
-
-    lax.fori_loop(0, chunks, sent, 0)
-    for h in range(PARTS):
-        for xx in range(X):
-            tok_copy(h, xx, False).wait_send()
-    for g in range(groups):
-        sums_back(g).wait_send()
-
-    def c_sent(j, carry):
-        c_copy(j).wait_send()
-        f_out(0, j).wait()
-        f_out(1, j).wait()
-        return carry
-
-    lax.fori_loop(0, pairs, c_sent, 0)
-    for way in range(2):
-        y_half(way).wait_send()
-        y_pair(way).wait_send()
-        f_pair(way, False).wait_send()
-        f_half(way, False).wait_send()
-    for d in range(-1, Y - 1):
-        fc_copy(d, False).wait_send()
-    z_copy().wait_send()
-    fz_copy(False).wait_send()
+    for k in range(len(kinds)):
+        moved(k, chunks - 1, False).wait_send()
+    sums_back(groups - 1).wait_send()
 
 
 def write_out(q_h, att, mast, mom, fresh, packed, bias, att_o, mast_o, mom_o, fresh_o, q, last, sem):
@@ -591,8 +608,8 @@
             pltpu.VMEM((groups, tok_count, 2 * HEAD), F32),
             pltpu.VMEM((groups, tok_count, 2 * HEAD), F32),
             pltpu.VMEM((tok_count, width // 4), BF),
-            dma((groups * PARTS, 9)),
-            dma((groups * PARTS, 9)),
+            dma((groups * PARTS, 12)),
+            dma((groups * PARTS, 12)),
             dma((PARTS, X)),
             dma((PARTS, X)),
             dma((groups,)),

time: 119 us -> 118 us (level)
  no operation moved by 1% of the time
where the time goes in v6:
time: 118 us
  Pallas kernels  117 us (99%)
    pallas_call x1, Pallas kernels, shards(): pl.pallas_call(kernel, out_shape=(pltpu.VMEM((tok_count, q_width - q_widt...  114 us
    pallas_call x1, Pallas kernels, shards(): pl.pallas_call(write_out, out_shape=(jax.ShapeDtypeStruct((tok_count, q_w...  3.05 us

profile of v6, /device:TPU:0, one launch (start us, length us, event | category | flops | bytes accessed | tf_op | source)
XLA Modules:
  0.0 118.2 jit_solution(8474190521895550984)
XLA Ops:
  0.6 0.0 copy-start
  0.6 114.4 %fused.1 = (bf16[384,3072]{1,0:T(8,128)(2,1)S(1)}, f32[192,512]{1,0:T(8,128)S(1)}, f32[192,512]{1,0:T(8,128)S(1)}, bf16[192,8192]{1,0:T(8,128)(2,1)S(1)}, bf16[3...) custom-call(bf16[384,8192]{1,0:T(8,128)(2,1)} %bitcast.8, bf16[384,4096]{1,0:T(8,128)(2,1)} %bitcast.6, ...), custom_call_target="tpu_custom_call" | custom-call | flops 8999999488 | bytes 30000000 | tf_op jit(solution)/shard_map/fused/pallas_call | solution.py:578
  115.1 0.0 copy-done
  115.1 3.1 %write_out.1 = (bf16[384,4096]{1,0:T(8,128)(2,1)}, f32[192,512]{1,0:T(8,128)}, f32[192,512]{1,0:T(8,128)}, bf16[192,8192]{1,0:T(8,128)(2,1)}) custom-call(bf16[384,4096]{1,0:T(8,128)(2,1)S(1)} %bitcast.7, bf16[384,3072]{1,0:T(8,128)(2,1)S(1)} %get-tuple-element.14.att, f32[192,512]{1,0:T(8,128)S(1)} %get-tuple-element.15.mast, ...), custom_call_target="tpu_custom_call" | custom-call | tf_op jit(solution)/shard_map/write_out/pallas_call | solution.py:641
Async XLA Ops:
  0.6 114.5 %copy-start = (bf16[1,384,4096]{2,1,0:T(8,128)(2,1)S(1)}, bf16[1,384,4096]{2,1,0:T(8,128)(2,1)}, u32[]{:S(2)}) copy-start(bf16[1,384,4096]{2,1,0:T(8,128)(2,1)} %param.9) | copy-start | bytes 9437188
